TPU v7x, 512 devices: a whole 4x4x16 slice. The times are simulated.
512 devices in a mesh: dp: 16 (over z_lo, core), expert: 32 (over y, z_hi, x).
Axes of the slice: x: 4, y: 4, z: 16 (z_hi: 2, z_lo: 8; z = z_hi * 8 + z_lo), core: 2. Of those that a mesh axis runs over, the one named last changes fastest.
Arguments:
- tokens: bfloat16 [65536, 1024], P(('dp', 'expert')), may hold values from -6 to 6
- cotangent: bfloat16 [65536, 1024], P(('dp', 'expert')), may hold values from -6 to 6
- routing: int32 [65536, 2], P(('dp', 'expert')), may hold values from 0 to 31, all different within a row; in each aligned block of 128 rows (0 to 127, 128 to 255, ...) at most 16 rows name the same one
- gate_values: float32 [65536, 2], P(('dp', 'expert')), may hold values from 0.1 to 1
- live_counts: int32 [512], P(('dp', 'expert')), may hold values from 64 to 128
- gate_weights: bfloat16 [32, 1024, 384], P('expert', 'dp'), may hold values from -0.1875 to 0.1875
- up_weights: bfloat16 [32, 1024, 384], P('expert', 'dp'), may hold values from -0.1875 to 0.1875
- down_weights: bfloat16 [32, 384, 1024], P('expert', 'dp'), may hold values from -0.3125 to 0.3125
Outputs:
- mixed: bfloat16 [65536, 1024], P(('dp', 'expert'))
- token_grad: bfloat16 [65536, 1024], P(('dp', 'expert'))
- gate_grad: float32 [65536, 2], P(('dp', 'expert'))
- grad_gate_w: bfloat16 [32, 1024, 384], P('expert', 'dp')
- grad_up_w: bfloat16 [32, 1024, 384], P('expert', 'dp')
- grad_down_w: bfloat16 [32, 384, 1024], P('expert', 'dp')
Inputs may be any that keep to these rules, and one draw needn't show every extreme that they name: `routing`: each row names 2 different experts; among the 128 rows of one device no expert is named by more than 16 rows.
All inputs are finite; a program needn't handle non-finite values.
Results may differ from a plain program's by a relative error of at most 0.018.
Values may be sent and summed in bfloat16 or wider, within the bound.
A program may use at most 64 MiB of HBM per device.

v0:
```python
import math

import jax
import jax.numpy as jnp
from jax import lax
from jax.sharding import PartitionSpec as P


def sent_together(arrays, axis, split_dim, concat_dim, along):
    both = jnp.concatenate(arrays, axis=along)
    out, at, gathered = (
        lax.all_to_all(both, axis, split_axis=split_dim, concat_axis=concat_dim, tiled=True),
        0,
        [],
    )
    for a in arrays:
        gathered.append(lax.slice_in_dim(out, at, at + a.shape[along], axis=along))
        at += a.shape[along]
    return tuple(gathered)


def sent_together_2(arrays, axis, dim, along):
    both = jnp.concatenate(arrays, axis=along)
    out, at, gathered = (lax.all_gather(both, axis, axis=dim, tiled=True), 0, [])
    for a in arrays:
        gathered.append(lax.slice_in_dim(out, at, at + a.shape[along], axis=along))
        at += a.shape[along]
    return tuple(gathered)


def split_up(shard, dim, devices):
    before, after = (shard.shape[:dim], shard.shape[dim + 1 :])
    return jnp.moveaxis(shard.reshape(*before, devices, -1, *after), dim, 0)


def sum_packed(arrays, axis, dims):
    devices = lax.axis_size(axis)
    pieces = [split_up(a, dim, devices) for a, dim in zip(arrays, dims)]
    lines = jnp.concatenate([b.reshape(devices, -1) for b in pieces], axis=1)
    width = max(16, -(-lines.shape[1] // 1024) * 8)
    lines = jnp.pad(lines, ((0, 0), (0, width * 128 - lines.shape[1]))).reshape(-1, 128)
    flat, at, gathered = (lax.psum_scatter(lines, axis, tiled=True).reshape(-1), 0, [])
    for b in pieces:
        part = b[0]
        gathered.append(flat[at : at + part.size].reshape(part.shape))
        at += part.size
    return tuple(gathered)


def contract_last(left, right):
    return lax.dot_general(
        left, right, (((1,), (1,)), ((), ())), preferred_element_type=jnp.float32
    )


def contract_first(left, right):
    return lax.dot_general(
        left, right, (((0,), (0,)), ((), ())), preferred_element_type=jnp.float32
    )


def expert_block(rows_in, grads_in, row_limit, weights, row_start, tile_rows):
    gate_w, up_w, down_w = weights
    tokens_blk = lax.dynamic_slice_in_dim(rows_in, row_start, tile_rows, 0)
    cot_blk = lax.dynamic_slice_in_dim(grads_in, row_start, tile_rows, 0)
    keep_rows = row_start + jnp.arange(tile_rows, dtype=jnp.int32) < row_limit
    cot_blk = jnp.where(keep_rows[:, None], cot_blk, jnp.zeros_like(cot_blk))
    pre_gate = jnp.dot(tokens_blk, gate_w, preferred_element_type=jnp.float32)
    pre_up = jnp.dot(tokens_blk, up_w, preferred_element_type=jnp.float32)
    sigmoid_gate = jax.nn.sigmoid(pre_gate)
    swish_gate = pre_gate * sigmoid_gate
    hidden = (swish_gate * pre_up).astype(jnp.bfloat16)
    outputs = jnp.dot(hidden, down_w, preferred_element_type=jnp.float32).astype(jnp.bfloat16)
    hidden_grad = contract_last(cot_blk, down_w)
    gate_pre = (
        hidden_grad * pre_up * sigmoid_gate * (1.0 + pre_gate * (1.0 - sigmoid_gate))
    ).astype(jnp.bfloat16)
    up_pre = (hidden_grad * swish_gate).astype(jnp.bfloat16)
    token_part = (contract_last(gate_pre, gate_w) + contract_last(up_pre, up_w)).astype(
        jnp.bfloat16
    )
    return (outputs, token_part, gate_pre, up_pre, hidden, tokens_blk, cot_blk)


def run_experts(rows_in, grads_in, row_limit, weights, tile_rows):
    total_rows, model_width = rows_in.shape

    def one_tile(tile_idx, state_now):
        outputs_all, parts_all, extra = state_now
        row_start = tile_idx * tile_rows
        outputs, token_part, gate_pre, up_pre, hidden, tokens_blk, cot_blk = expert_block(
            rows_in, grads_in, row_limit, weights, row_start, tile_rows
        )
        outputs_all = lax.dynamic_update_slice_in_dim(outputs_all, outputs, row_start, 0)
        parts_all = lax.dynamic_update_slice_in_dim(parts_all, token_part, row_start, 0)
        grads = (
            contract_first(tokens_blk, gate_pre),
            contract_first(tokens_blk, up_pre),
            contract_first(hidden, cot_blk),
        )
        extra = tuple((first + second for first, second in zip(extra, grads)))
        return (outputs_all, parts_all, extra)

    tile_count = (row_limit + tile_rows - 1) // tile_rows
    extra_init = tuple((jnp.zeros(piece.shape, jnp.float32) for piece in weights))
    initial = (
        jnp.zeros((total_rows, model_width), jnp.bfloat16),
        jnp.zeros((total_rows, model_width), jnp.bfloat16),
        extra_init,
    )
    return lax.fori_loop(jnp.int32(0), tile_count, one_tile, initial)


def shards(
    tokens, cotangent, routing, gate_values, live_counts, gate_weights, up_weights, down_weights
):
    experts = lax.axis_size("expert")
    groups = lax.axis_size("dp")
    tok_rows, model_width = tokens.shape
    top_count = routing.shape[1]
    capacity = 2 * tok_rows * top_count // experts
    recv_rows = experts * capacity
    help_rows = recv_rows // 4
    tile_rows = math.gcd(128, help_rows)
    assigned = tok_rows * top_count
    padded_rows = recv_rows + help_rows
    alive_rows = jnp.arange(tok_rows, dtype=jnp.int32) < live_counts[0]
    alive_flat = jnp.repeat(alive_rows, top_count)
    target = routing.reshape(-1)
    onehot = (
        (target[:, None] == jnp.arange(experts, dtype=jnp.int32)[None, :]) & alive_flat[:, None]
    ).astype(jnp.int32)
    before = jnp.cumsum(onehot, axis=0) - onehot
    position = jnp.sum(before * onehot, axis=1)
    slot_index = jnp.where(alive_flat, target * capacity + position, recv_rows)
    slot_source = (
        jnp.full((recv_rows + 1,), assigned, jnp.int32)
        .at[slot_index]
        .set(jnp.arange(assigned, dtype=jnp.int32))[:recv_rows]
    )
    token_of = slot_source // top_count
    tokens_pad = jnp.concatenate([tokens, jnp.zeros((1, model_width), tokens.dtype)], 0)
    cot_pad = jnp.concatenate([cotangent, jnp.zeros((1, model_width), cotangent.dtype)], 0)
    gates_pad = jnp.concatenate([gate_values.reshape(-1), jnp.zeros((1,), jnp.float32)], 0)
    send_rows = tokens_pad[token_of]
    send_grads = (gates_pad[slot_source][:, None] * cot_pad[token_of]).astype(jnp.bfloat16)
    per_target = jnp.sum(onehot, axis=0).reshape(experts, 1)
    recv_tokens, recv_grads, recv_counts = (
        *sent_together(
            (
                send_rows.reshape(experts, capacity, model_width),
                send_grads.reshape(experts, capacity, model_width),
            ),
            "expert",
            0,
            0,
            1,
        ),
        lax.all_to_all(per_target, "expert", split_axis=0, concat_axis=0, tiled=True),
    )
    recv_tokens = recv_tokens.reshape(recv_rows, model_width)
    recv_grads = recv_grads.reshape(recv_rows, model_width)
    in_slot = jnp.arange(recv_rows, dtype=jnp.int32) % capacity < jnp.repeat(
        recv_counts[:, 0], capacity
    )
    slot_flags = in_slot.astype(jnp.int32)
    packed_at = jnp.cumsum(slot_flags) - slot_flags
    own_load = jnp.sum(slot_flags)
    pack_order = (
        jnp.full((padded_rows,), recv_rows, jnp.int32)
        .at[jnp.where(in_slot, packed_at, padded_rows)]
        .set(jnp.arange(recv_rows, dtype=jnp.int32), mode="drop")
    )
    zero_row = jnp.zeros((1, model_width), jnp.bfloat16)
    packed_tokens = jnp.concatenate([recv_tokens, zero_row], 0)[pack_order]
    packed_grads = jnp.concatenate([recv_grads, zero_row], 0)[pack_order]
    gathered = (
        *sent_together_2((gate_weights, up_weights), "dp", 1, 0),
        lax.all_gather(down_weights, "dp", axis=1, tiled=True),
    )
    own_weights = (gathered[0][0], gathered[1][0], gathered[2][0])
    outputs_all, parts_all, grad_sums = run_experts(
        packed_tokens, packed_grads, own_load, own_weights, tile_rows
    )
    take_from = jnp.where(in_slot, packed_at, padded_rows)
    slot_out = jnp.concatenate([outputs_all, zero_row], 0)[take_from]
    slot_parts = jnp.concatenate([parts_all, zero_row], 0)[take_from]
    back_tokens, back_token_parts = sent_together(
        (
            slot_out.reshape(experts, capacity, model_width),
            slot_parts.reshape(experts, capacity, model_width),
        ),
        "expert",
        0,
        0,
        1,
    )
    flat_out = jnp.concatenate([back_tokens.reshape(recv_rows, model_width), zero_row], 0)[
        slot_index
    ]
    flat_parts = jnp.concatenate([back_token_parts.reshape(recv_rows, model_width), zero_row], 0)[
        slot_index
    ]
    expert_out = flat_out.reshape(tok_rows, top_count, model_width)
    mixed = jnp.sum(gate_values[:, :, None] * expert_out, axis=1).astype(jnp.bfloat16)
    gate_grad = jnp.einsum("td,tkd->tk", cotangent, expert_out, preferred_element_type=jnp.float32)
    token_grad = jnp.sum(
        flat_parts.reshape(tok_rows, top_count, model_width).astype(jnp.float32), axis=1
    ).astype(jnp.bfloat16)
    reduced = tuple(
        (
            part.astype(jnp.float32)
            for part in sum_packed(
                (
                    grad_sums[0][None].astype(jnp.bfloat16),
                    grad_sums[1][None].astype(jnp.bfloat16),
                    grad_sums[2][None].astype(jnp.bfloat16),
                ),
                "dp",
                (1, 1, 1),
            )
        )
    )
    grad_gate_w = (reduced[0] / groups).astype(jnp.bfloat16)
    grad_up_w = (reduced[1] / groups).astype(jnp.bfloat16)
    grad_down_w = (reduced[2] / groups).astype(jnp.bfloat16)
    return (mixed, token_grad, gate_grad, grad_gate_w, grad_up_w, grad_down_w)


def solution(mesh):
    return jax.shard_map(
        shards,
        mesh=mesh,
        in_specs=(
            P(("dp", "expert"), None),
            P(("dp", "expert"), None),
            P(("dp", "expert"), None),
            P(("dp", "expert"), None),
            P(("dp", "expert")),
            P("expert", "dp", None),
            P("expert", "dp", None),
            P("expert", "dp", None),
        ),
        out_specs=(
            P(("dp", "expert"), None),
            P(("dp", "expert"), None),
            P(("dp", "expert"), None),
            P("expert", "dp", None),
            P("expert", "dp", None),
            P("expert", "dp", None),
        ),
        check_vma=False,
    )
```

profile of v0, /device:TPU:1, one launch (start us, length us, event | category | flops | bytes accessed | tf_op | source)
XLA Modules:
  0.0 452.2 jit_solution(5627230513921606627)
XLA Ops:
  11.1 21.1 %all-to-all-start = ((s32[32,1,1]{2,1,0:T(1,128)}), s32[32,1,1]{2,1,0:T(1,128)S(1)}, u32[]{:S(2)}, u32[]{:S(2)}) async-start(s32[32,1,1]{2,1,0:T(1,128)} %copy.30), calls=%async_computation | async-start | bytes 32768 | tf_op jit(solution)/shard_map/all_to_all | solution.py:159
  33.4 1.4 scatter_custom_fusion
  35.8 3.5 gather_fusion.1
  39.4 2.1 gather_fusion.2
  41.5 2.1 gather_fusion
  43.8 1.7 pad_maximum_fusion.1
  45.5 2.6 all-to-all-done
  48.0 14.1 %all-to-all-start.1 = ((bf16[32,32,1024]{2,1,0:T(8,128)(2,1)}), bf16[32,32,1024]{2,1,0:T(8,128)(2,1)}, u32[]{:S(2)}, u32[]{:S(2)}) async-start(bf16[32,32,1024]{2,1,0:T(8,128)(2,1)} %pad_maximum_fusion.1), calls=%async_computation.1 | async-start | bytes 4194304 | tf_op jit(solution)/shard_map/all_to_all | solution.py:12
  63.0 128.1 %all_gather.7 = bf16[1,384,1024]{2,1,0:T(8,128)(2,1)} all-gather(bf16[1,24,1024]{2,1,0:T(8,128)(2,1)S(1)} %copy-done.10), channel_id=1, replica_groups=mesh['dp'=16,'expert'=32] {'dp'}, dimensions={1}, use_global_device_ids=true | all-gather | bytes 835584 | tf_op jit(solution)/shard_map/all_gather | solution.py:179
  194.1 2.4 scatter_custom_fusion.1
  196.6 4.4 all-gather.2.cloned.1.call-done
  201.0 1.5 slice_bitcast_fusion
  202.5 2.8 fusion.40
  205.4 3.5 gather_fusion.3
  208.8 1.3 concatenate.45
  210.1 3.5 gather_fusion.4
  213.8 1.3 broadcast.266.clone
  215.0 1.3 broadcast_in_dim.66
  216.4 1.2 broadcast.265
  217.6 1.2 broadcast.265.clone
  218.8 26.4 %while.18 = (s32[]{:T(128)}, bf16[640,1024]{1,0:T(8,128)(2,1)}, bf16[640,1024]{1,0:T(8,128)(2,1)}, f32[1024,384]{1,0:T(8,128)S(1)}, f32[1024,384]{1,0:T(8,128)},...) while((s32[]{:T(128)}, bf16[640,1024]{1,0:T(8,128)(2,1)}, ...), condition=%wide.region_10.11_spmd, body=%wide.region_9.10_spmd.sunk | while | flops 908542208 | bytes 34702024 | solution.py:111
  218.8 1.3 fusion.92
  220.2 1.3 fusion.93
  222.1 1.4 multiply_convert_fusion.7
  224.9 1.4 convolution_add_fusion.9
  226.3 1.6 convolution_add_fusion.7
  227.9 3.1 convolution_add_fusion.8
  232.0 1.3 fusion.92
  233.4 1.2 fusion.93
  235.3 1.3 multiply_convert_fusion.7
  238.1 1.4 convolution_add_fusion.9
  239.5 1.6 convolution_add_fusion.7
  241.2 3.1 convolution_add_fusion.8
  245.3 2.5 convert_element_type.162
  247.8 2.4 reshape_transpose_reshape.10
  251.2 2.4 reshape_transpose_reshape.11
  253.6 1.3 reshape_transpose_reshape.9
  254.9 1.4 concatenate.46
  256.3 2.8 gather_fusion.5
  259.2 2.1 gather_fusion.6
  261.3 1.6 pad_maximum_fusion.2
  262.9 30.1 %all-to-all-start.2 = ((bf16[32,32,1024]{2,1,0:T(8,128)(2,1)}), bf16[32,32,1024]{2,1,0:T(8,128)(2,1)}, u32[]{:S(2)}, u32[]{:S(2)}) async-start(bf16[32,32,1024]{2,1,0:T(8,128)(2,1)} %pad_maximum_fusion.2), calls=%async_computation.2 | async-start | bytes 4194304 | tf_op jit(solution)/shard_map/all_to_all | solution.py:12
  293.4 1.5 pad_maximum_fusion
  294.9 2.1 reshape.347
  297.1 134.7 %reduce-scatter.2.cloned.1.call-done = bf16[576,128]{1,0:T(8,128)(2,1)} async-done(((bf16[9216,128]{1,0:T(8,128)(2,1)}), bf16[576,128]{1,0:T(8,128)(2,1)}) %reduce-scatter.2.cloned.1.call-update) | async-done | bytes 147472 | tf_op jit(solution)/shard_map/reduce_scatter | solution.py:42
  434.6 1.8 fusion.39
  439.3 2.1 multiply_reduce_fusion
  443.2 2.1 reduce_sum.55
  (115 shorter events, 24.3 us)
Async XLA Ops:
  7.2 32.2 %copy-start.8 = (bf16[128,1024]{1,0:T(8,128)(2,1)S(1)}, bf16[128,1024]{1,0:T(8,128)(2,1)}, u32[]{:S(2)}) copy-start(bf16[128,1024]{1,0:T(8,128)(2,1)} %param.11) | copy-start | bytes 786436
  11.1 36.9 %all-to-all-start = ((s32[32,1,1]{2,1,0:T(1,128)}), s32[32,1,1]{2,1,0:T(1,128)S(1)}, u32[]{:S(2)}, u32[]{:S(2)}) async-start(s32[32,1,1]{2,1,0:T(1,128)} %copy.30), calls=%async_computation | async-start | bytes 32768 | tf_op jit(solution)/shard_map/all_to_all | solution.py:159
  39.4 2.1 copy-start.7
  45.5 16.8 %copy-start.11 = (bf16[1,64,384]{2,1,0:T(8,128)(2,1)S(1)}, bf16[1,64,384]{2,1,0:T(8,128)(2,1)}, u32[]{:S(2)}) copy-start(bf16[1,64,384]{2,1,0:T(8,128)(2,1)} %param.16) | copy-start | bytes 147460
  45.5 16.8 %copy-start.12 = (bf16[1,64,384]{2,1,0:T(8,128)(2,1)S(1)}, bf16[1,64,384]{2,1,0:T(8,128)(2,1)}, u32[]{:S(2)}) copy-start(bf16[1,64,384]{2,1,0:T(8,128)(2,1)} %param.15) | copy-start | bytes 147460
  45.5 17.5 %copy-start.10 = (bf16[1,24,1024]{2,1,0:T(8,128)(2,1)S(1)}, bf16[1,24,1024]{2,1,0:T(8,128)(2,1)}, u32[]{:S(2)}) copy-start(bf16[1,24,1024]{2,1,0:T(8,128)(2,1)} %param.17) | copy-start | bytes 147460
  48.0 154.5 %all-to-all-start.1 = ((bf16[32,32,1024]{2,1,0:T(8,128)(2,1)}), bf16[32,32,1024]{2,1,0:T(8,128)(2,1)}, u32[]{:S(2)}, u32[]{:S(2)}) async-start(bf16[32,32,1024]{2,1,0:T(8,128)(2,1)} %pad_maximum_fusion.1), calls=%async_computation.1 | async-start | bytes 4194304 | tf_op jit(solution)/shard_map/all_to_all | solution.py:12
  62.2 138.8 %all-gather.2.cloned.1.call-start = ((), (), s32[]{:S(2)}) async-start(), calls=%async_computation.4 | async-start | bytes 1671168 | tf_op jit(solution)/shard_map/all_gather | solution.py:24
  218.8 3.2 copy-start.3
  223.4 1.5 copy-start
  226.3 1.6 copy-start.1
  232.0 3.2 copy-start.3
  236.6 1.5 copy-start
  239.5 1.6 copy-start.1
  245.3 4.9 %copy-start.2 = (f32[384,1024]{1,0:T(8,128)S(1)}, f32[384,1024]{1,0:T(8,128)}, u32[]{:S(2)}) copy-start(f32[384,1024]{1,0:T(8,128)} %get-tuple-element.82) | copy-start | bytes 4718596
  256.3 2.8 copy-start.4
  259.2 2.1 copy-start.5
  262.9 30.4 %copy-start.6 = (bf16[16,24576]{1,0:T(8,128)(2,1)S(1)}, bf16[16,24576]{1,0:T(8,128)(2,1)}, u32[]{:S(2)}) copy-start(bf16[16,24576]{1,0:T(8,128)(2,1)} %reshape_transpose_reshape.10) | copy-start | bytes 2359300
  262.9 171.7 %all-to-all-start.2 = ((bf16[32,32,1024]{2,1,0:T(8,128)(2,1)}), bf16[32,32,1024]{2,1,0:T(8,128)(2,1)}, u32[]{:S(2)}, u32[]{:S(2)}) async-start(bf16[32,32,1024]{2,1,0:T(8,128)(2,1)} %pad_maximum_fusion.2), calls=%async_computation.2 | async-start | bytes 4194304 | tf_op jit(solution)/shard_map/all_to_all | solution.py:12
  293.1 138.7 %reduce-scatter.2.cloned.1.call-start = ((), (), s32[]{:S(2)}) async-start(), calls=%async_computation.5 | async-start | bytes 2506752 | tf_op jit(solution)/shard_map/reduce_scatter | solution.py:42
  439.1 2.4 copy-start.9
Sparse Core Ops, SparseCore 0:
  65.7 135.2 all-gather.1
  297.2 134.5 reduce-scatter.1
where the time goes:
time: 457 us; the launch traced here: 452 us
  waiting for transfers between devices  142 us (31%)
  blocking collectives  128 us (28%)
  starting transfers between devices  65.7 us (14%)
  local copies, waits for them, and re-layouts  55.6 us (12%)
  matrix products  26.1 us (6%)
  other arithmetic  19.1 us (4%)
  between operations  15.8 us (3%)
    reduce_scatter x1, waiting for transfers between devices, sum_packed(): lax.psum_scatter(lines, axis, tiled=True).reshape(-1)  135 us
    all_gather x1, blocking collectives, shards(): lax.all_gather(down_weights, 'dp', axis=1, tiled=True)  128 us
    all_to_all x2, starting transfers between devices, sent_together(): lax.all_to_all(both, axis, split_axis=split_dim, concat_axis=concat_dim,...  44.3 us
    all_to_all x1, starting transfers between devices, shards(): lax.all_to_all(per_target, 'expert', split_axis=0, concat_axis=0, tiled=T...  21.1 us
    dot_general x6, matrix products, contract_first(): lax.dot_general(left, right, (((0,), (0,)), ((), ())), preferred_element_...  12.1 us
  transfers between devices with their start and end apart: 5, of which 3 were waited for; matrix products, arithmetic and copies ran while one was open for 6% of the time, Pallas kernels for 0%

commit v1 on v0

v1 whole, which is shorter than its diff:
```python
import functools

import jax
import jax.numpy as jnp
from jax import lax
from jax.experimental import pallas as pl
from jax.experimental.pallas import tpu as pltpu
from jax.sharding import PartitionSpec as P

NX, NY, NZL = 4, 4, 8
CAP = 16
BF, F32 = jnp.bfloat16, jnp.float32


def contract_last(left, right):
    return lax.dot_general(
        left, right, (((1,), (1,)), ((), ())), preferred_element_type=F32
    )


def contract_first(left, right):
    return lax.dot_general(
        left, right, (((0,), (0,)), ((), ())), preferred_element_type=F32
    )


def dot(left, right):
    return jnp.dot(left, right, preferred_element_type=F32)


def kernel(
    tok, cot, routing, gates, live,
    gate_in, up_in, down_in,
    mixed, token_grad, gate_grad, out_g, out_u, out_d,
    wg, wu, wd, down_full,
    send_x, send_c, recv_x, recv_c,
    send_o, send_p, back_o, back_p,
    hidden, pre_grads,
    own_g, own_u, own_d, sum_g, sum_u, sum_d, fin_g, fin_u, fin_d, land_g, land_u, land_d,
    ag_send, ag_recv, push_send, push_recv,
    rs_send, rs_recv, fin_send, fin_recv,
    a2a_send, a2a_recv, back_send, back_recv,
):
    rows_tok, width = tok.shape
    planes = 2 * NX * NY
    nz = 2 * NZL
    slots = planes * CAP
    ff = gate_in.shape[-1]

    dp, ex = lax.axis_index("dp"), lax.axis_index("expert")
    zl, c = lax.div(dp, 2), lax.rem(dp, 2)
    y, zh, x = lax.div(ex, 2 * NX), lax.rem(lax.div(ex, NX), 2), lax.rem(ex, NX)
    z = zh * NZL + zl
    me = y * (2 * NX) + c * NX + x

    def along_z(zz, core):
        return (lax.rem(zz, NZL) * 2 + core, y * (2 * NX) + lax.div(zz, NZL) * NX + x)

    def in_plane(q):
        qy, qc, qx = lax.div(q, 2 * NX), lax.rem(lax.div(q, NX), 2), lax.rem(q, NX)
        return (zl * 2 + qc, qy * (2 * NX) + zh * NX + qx)

    ring = (along_z(lax.rem(z + 1, nz), c), along_z(lax.rem(z + nz - 1, nz), c))
    other = along_z(z, 1 - c)
    reach = (NZL, NZL - 1)

    def remote(src, dst, send_sem, recv_sem, device):
        return pltpu.make_async_remote_copy(
            src_ref=src, dst_ref=dst, send_sem=send_sem, recv_sem=recv_sem,
            device_id=device, device_id_type=pl.DeviceIdType.MESH,
        )

    barrier = pltpu.get_barrier_semaphore()

    def greet(o, _):
        pl.semaphore_signal(
            barrier, inc=1, device_id=in_plane(lax.rem(me + o, planes)),
            device_id_type=pl.DeviceIdType.MESH,
        )
        return 0

    for device in ring:
        pl.semaphore_signal(
            barrier, inc=1, device_id=device, device_id_type=pl.DeviceIdType.MESH
        )
    lax.fori_loop(1, planes, greet, 0)
    pl.semaphore_wait(barrier, planes + 1)

    shards_in = (gate_in, up_in, down_in)
    weights = (wg, wu, wd)

    def push(q):
        return remote(
            shards_in[q].at[0], weights[q].at[dp], push_send.at[q], push_recv.at[q], other
        )

    def ag_copy(q, flow, block):
        at = weights[q].at[pl.ds(2 * block, 2)]
        return remote(at, at, ag_send.at[flow, block, q], ag_recv.at[block, q], ring[flow])

    def source(flow, hops):
        zz = lax.rem(z - hops + nz, nz) if flow == 0 else lax.rem(z + hops, nz)
        return lax.rem(zz, NZL), lax.div(zz, NZL) == c

    @pl.when(zh != c)
    def _():
        for q in range(3):
            push(q).start()

    @pl.when(zh == c)
    def _():
        for q in range(3):
            weights[q][dp] = shards_in[q][0]
        for q in range(3):
            pltpu.make_async_copy(weights[q].at[dp], weights[q].at[dp], push_recv.at[q]).wait()
            for flow in (0, 1):
                ag_copy(q, flow, zl).start()

    eye = lax.broadcasted_iota(jnp.int32, (rows_tok, rows_tok), 0) == lax.broadcasted_iota(
        jnp.int32, (rows_tok, rows_tok), 1
    )

    def column(row):
        return jnp.sum(jnp.where(eye, row, 0.0), axis=1, keepdims=True)

    def row_of(col):
        return jnp.sum(jnp.where(eye, col, 0.0), axis=0, keepdims=True)

    alive = lax.broadcasted_iota(jnp.int32, (rows_tok, 1), 0) < live[0]
    lanes = lax.broadcasted_iota(jnp.int32, (rows_tok, planes), 1).astype(F32)
    earlier = (
        lax.broadcasted_iota(jnp.int32, (rows_tok, rows_tok), 1)
        < lax.broadcasted_iota(jnp.int32, (rows_tok, rows_tok), 0)
    ).astype(BF)
    slot, weight = [], []
    taken = jnp.zeros((1, planes), F32)
    for k in range(2):
        expert = column(routing[k : k + 1, :].astype(F32))
        weight.append(column(gates[k : k + 1, :]))
        onehot = jnp.where((expert == lanes) & alive, 1.0, 0.0)
        before = dot(earlier, onehot.astype(BF)) + taken
        taken = taken + jnp.sum(onehot, axis=0, keepdims=True)
        found = jnp.sum(onehot * (before + lanes * CAP), axis=1, keepdims=True)
        slot.append(jnp.where(alive, found, -1.0).astype(jnp.int32))

    def picks(k, start, count):
        at = lax.broadcasted_iota(jnp.int32, (rows_tok, count), 1) + start
        return jnp.where(slot[k] == at, 1.0, 0.0).astype(BF)

    scaled = [(weight[k] * cot[...].astype(F32)).astype(BF) for k in range(2)]

    def dispatch(q):
        return (
            remote(send_x.at[q], recv_x.at[me], a2a_send.at[0], a2a_recv.at[0], in_plane(q)),
            remote(send_c.at[q], recv_c.at[me], a2a_send.at[1], a2a_recv.at[1], in_plane(q)),
        )

    group = 2 * NX
    for j in range(NY):
        first = lax.rem(y + j, NY) * group
        p0, p1 = (picks(k, first * CAP, group * CAP) for k in range(2))
        shape = (group, CAP, width)
        send_x[pl.ds(first, group)] = contract_first(p0 + p1, tok[...]).astype(BF).reshape(shape)
        send_c[pl.ds(first, group)] = (
            (contract_first(p0, scaled[0]) + contract_first(p1, scaled[1])).astype(BF).reshape(shape)
        )

        def send(o, _, first=first):
            q = first + lax.rem(x + o, group)

            @pl.when(q != me)
            def _():
                for copy in dispatch(q):
                    copy.start()

            return 0

        lax.fori_loop(0, group, send, 0)
    recv_x[me] = send_x[me]
    recv_c[me] = send_c[me]

    def forward(s, _):
        for q in range(3):
            for flow in (0, 1):
                block, ours = source(flow, s)

                @pl.when(ours & (s <= reach[flow]))
                def _(q=q, flow=flow, block=block):
                    ag_copy(q, flow, block).wait_recv()

                    @pl.when(s < reach[flow])
                    def _():
                        ag_copy(q, flow, block).start()

        return 0

    lax.fori_loop(1, NZL + 1, forward, 0)

    shard_rows = down_in.shape[1]
    for i in range(nz):
        down_full[i * shard_rows : (i + 1) * shard_rows] = wd[i]

    def all_of(ref, sem, count):
        part = ref.at[pl.ds(0, count)]
        pltpu.make_async_copy(part, part, sem).wait()

    all_of(recv_x, a2a_recv.at[0], planes - 1)
    all_of(recv_c, a2a_recv.at[1], planes - 1)

    tiles = 2
    per = planes // tiles
    tile_rows = per * CAP

    def combine(q):
        return (
            remote(send_o.at[q], back_o.at[me], back_send.at[0], back_recv.at[0], in_plane(q)),
            remote(send_p.at[q], back_p.at[me], back_send.at[1], back_recv.at[1], in_plane(q)),
        )

    def tile(t, _):
        first = lax.rem(lax.div(y * tiles, NY) + t, tiles) * per
        rows = pl.multiple_of(first * CAP, tile_rows)
        xs = recv_x[pl.ds(first, per)].reshape(tile_rows, width)
        cs = recv_c[pl.ds(first, per)].reshape(tile_rows, width)
        gate_w = wg[...].reshape(width, ff)
        up_w = wu[...].reshape(width, ff)
        down_w = down_full[...]
        pre_gate = dot(xs, gate_w)
        pre_up = dot(xs, up_w)
        sig = jax.nn.sigmoid(pre_gate)
        swish = pre_gate * sig
        hid = (swish * pre_up).astype(BF)
        hidden[pl.ds(rows, tile_rows)] = hid
        send_o[pl.ds(first, per)] = dot(hid, down_w).astype(BF).reshape(per, CAP, width)
        hidden_grad = contract_last(cs, down_w)
        gate_pre = (hidden_grad * pre_up * sig * (1.0 + pre_gate * (1.0 - sig))).astype(BF)
        up_pre = (hidden_grad * swish).astype(BF)
        pre_grads[pl.ds(rows, tile_rows), :ff] = gate_pre
        pre_grads[pl.ds(rows, tile_rows), ff:] = up_pre
        part = contract_last(gate_pre, gate_w) + contract_last(up_pre, up_w)
        send_p[pl.ds(first, per)] = part.astype(BF).reshape(per, CAP, width)

        def send(o, _):
            q = first + lax.rem(group * (y % 2) + x + o, per)

            @pl.when(q != me)
            def _():
                for copy in combine(q):
                    copy.start()

            return 0

        lax.fori_loop(0, per, send, 0)
        return 0

    lax.fori_loop(0, tiles, tile, 0)
    back_o[me] = send_o[me]
    back_p[me] = send_p[me]

    own, sums = (own_g, own_u, own_d), (sum_g, sum_u, sum_d)
    both = contract_first(recv_x[...].reshape(slots, width), pre_grads[...])
    own_g[...] = both[:, :ff].astype(BF).reshape(own_g.shape)
    own_u[...] = both[:, ff:].astype(BF).reshape(own_u.shape)
    down_grad = contract_first(hidden[...], recv_c[...].reshape(slots, width))
    for i in range(nz):
        own_d[i] = down_grad[i * shard_rows : (i + 1) * shard_rows].astype(BF)

    def rs_copy(q, flow, block, src):
        at = sums[q].at[flow, pl.ds(2 * block, 2)]
        return remote(src, at, rs_send.at[flow, block, q], rs_recv.at[flow, block, q], ring[flow])

    def target(flow, hops):
        return source(1 - flow, hops)

    def summing(s, _):
        for q in range(3):
            for flow in (0, 1):
                left = reach[flow] - s
                block, ours = target(flow, left)
                here = pl.ds(2 * block, 2)

                @pl.when(ours & (left > 0))
                def _(q=q, flow=flow, block=block, here=here):
                    @pl.when(s == 0)
                    def _():
                        rs_copy(q, flow, block, own[q].at[here]).start()

                    @pl.when(s > 0)
                    def _():
                        at = sums[q].at[flow, here]
                        rs_copy(q, flow, block, at).wait_recv()
                        sums[q][flow, here] = (
                            sums[q][flow, here].astype(F32) + own[q][here].astype(F32)
                        ).astype(BF)
                        rs_copy(q, flow, block, at).start()

        return 0

    lax.fori_loop(0, NZL, summing, 0)

    all_of(back_o, back_recv.at[0], planes - 1)
    all_of(back_p, back_recv.at[1], planes - 1)
    p0, p1 = (picks(k, 0, slots) for k in range(2))
    token_grad[...] = dot(p0 + p1, back_p[...].reshape(slots, width)).astype(BF)
    total = jnp.zeros((rows_tok, width), F32)
    cot_f = cot[...].astype(F32)
    for k, p in enumerate((p0, p1)):
        got = dot(p, back_o[...].reshape(slots, width))
        total += weight[k] * got
        gate_grad[k : k + 1, :] = row_of(jnp.sum(cot_f * got, axis=1, keepdims=True))
    mixed[...] = total.astype(BF)

    outs, fins, lands = (out_g, out_u, out_d), (fin_g, fin_u, fin_d), (land_g, land_u, land_d)

    def fin_copy(q):
        return remote(fins[q].at[1 - c], lands[q], fin_send.at[q], fin_recv.at[q], other)

    @pl.when(zh == c)
    def _():
        here = pl.ds(2 * zl, 2)
        for q in range(3):
            for flow in (0, 1):
                at = sums[q].at[flow, here]
                rs_copy(q, flow, zl, at).wait_recv()
            fins[q][...] = (
                (
                    own[q][here].astype(F32)
                    + sums[q][0, here].astype(F32)
                    + sums[q][1, here].astype(F32)
                )
                * (1.0 / nz)
            ).astype(BF)
            fin_copy(q).start()
            outs[q][0] = fins[q][c]
        for q in range(3):
            fin_copy(q).wait_send()

    @pl.when(zh != c)
    def _():
        for q in range(3):
            fin_copy(q).wait_recv()
            outs[q][0] = lands[q][...]

    @pl.when(zh != c)
    def _():
        for q in range(3):
            push(q).wait_send()

    def sent(s, _):
        for q in range(3):
            for flow in (0, 1):
                block, ours = source(flow, s)

                @pl.when(ours & (s < reach[flow]))
                def _(q=q, flow=flow, block=block):
                    ag_copy(q, flow, block).wait_send()

                block, ours = target(flow, s + 1)

                @pl.when(ours & (s < reach[flow]))
                def _(q=q, flow=flow, block=block):
                    rs_copy(q, flow, block, own[q].at[pl.ds(2 * block, 2)]).wait_send()

        return 0

    lax.fori_loop(0, NZL, sent, 0)
    for ref, sem in (
        (send_x, a2a_send.at[0]),
        (send_c, a2a_send.at[1]),
        (send_o, back_send.at[0]),
        (send_p, back_send.at[1]),
    ):
        all_of(ref, sem, planes - 1)


def shards(
    tokens, cotangent, routing, gate_values, live_counts, gate_weights, up_weights, down_weights
):
    rows_tok, width = tokens.shape
    ff = gate_weights.shape[-1]
    planes, nz = 2 * NX * NY, 2 * NZL
    slots = planes * CAP
    shapes = [gate_weights.shape[1:], up_weights.shape[1:], down_weights.shape[1:]]
    vmem = pl.BlockSpec(memory_space=pltpu.VMEM)
    dma = pltpu.SemaphoreType.DMA
    block = pltpu.VMEM((planes, CAP, width), BF)
    flops = 18 * slots * width * ff
    outs = pl.pallas_call(
        kernel,
        out_shape=(
            jax.ShapeDtypeStruct((rows_tok, width), BF),
            jax.ShapeDtypeStruct((rows_tok, width), BF),
            jax.ShapeDtypeStruct((2, rows_tok), F32),
            *(jax.ShapeDtypeStruct((1, *s), BF) for s in shapes),
        ),
        in_specs=[vmem] * 4 + [pl.BlockSpec(memory_space=pltpu.SMEM)] + [vmem] * 3,
        out_specs=tuple([vmem] * 6),
        scratch_shapes=[
            *(pltpu.VMEM((nz, *s), BF) for s in shapes),
            pltpu.VMEM((ff, width), BF),
            *([block] * 8),
            pltpu.VMEM((slots, ff), BF),
            pltpu.VMEM((slots, 2 * ff), BF),
            *(pltpu.VMEM((nz, *s), BF) for s in shapes),
            *(pltpu.VMEM((2, nz, *s), BF) for s in shapes),
            *(pltpu.VMEM((2, *s), BF) for s in shapes),
            *(pltpu.VMEM(s, BF) for s in shapes),
            dma((2, NZL, 3)),
            dma((NZL, 3)),
            dma((3,)),
            dma((3,)),
            dma((2, NZL, 3)),
            dma((2, NZL, 3)),
            dma((3,)),
            dma((3,)),
            dma((2,)),
            dma((2,)),
            dma((2,)),
            dma((2,)),
        ],
        compiler_params=pltpu.CompilerParams(
            collective_id=0, has_side_effects=True, vmem_limit_bytes=56 * 1024 * 1024
        ),
        cost_estimate=pl.CostEstimate(
            flops=flops, bytes_accessed=2 * 1024 * 1024, transcendentals=slots * ff
        ),
    )(
        tokens, cotangent, routing.T, gate_values.T, live_counts,
        gate_weights, up_weights, down_weights,
    )
    mixed, token_grad, gate_grad, grad_g, grad_u, grad_d = outs
    return mixed, token_grad, gate_grad.T, grad_g, grad_u, grad_d


def solution(mesh):
    return jax.shard_map(
        shards,
        mesh=mesh,
        in_specs=(
            P(("dp", "expert"), None),
            P(("dp", "expert"), None),
            P(("dp", "expert"), None),
            P(("dp", "expert"), None),
            P(("dp", "expert")),
            P("expert", "dp", None),
            P("expert", "dp", None),
            P("expert", "dp", None),
        ),
        out_specs=(
            P(("dp", "expert"), None),
            P(("dp", "expert"), None),
            P(("dp", "expert"), None),
            P("expert", "dp", None),
            P("expert", "dp", None),
            P("expert", "dp", None),
        ),
        check_vma=False,
    )
```

time: 457 us -> 108 us (0.24)
  waiting for transfers between devices: 142 us -> 0 us
  blocking collectives: 128 us -> 0 us
  Pallas kernels: 0 us -> 101 us
  starting transfers between devices: 65.7 us -> 0 us
  local copies, waits for them, and re-layouts: 55.6 us -> 5.24 us
  matrix products: 26.1 us -> 0 us
  other arithmetic: 19.1 us -> 0 us
  between operations: 15.8 us -> 1.3 us
    reduce_scatter x1 -> x0, waiting for transfers between devices: 135 us -> none  [sum_packed(): lax.psum_scatter(lines, axis, tiled=True).reshape(-1)]
    all_gather x1 -> x0, blocking collectives: 128 us -> none  [shards(): lax.all_gather(down_weights, 'dp', axis=1, tiled=True)]
    pallas_call x0 -> x1, Pallas kernels: none -> 101 us  [shards(): pl.pallas_call(kernel, out_shape=(jax.ShapeDtypeStruct((rows_tok, width),...]
    all_to_all x3 -> x0, starting transfers between devices: 65.4 us -> none  [the longest x2 44.3 us: sent_together(): lax.all_to_all(both, axis, split_axis=split_dim, concat_axis=concat_dim,...]
    dot_general x19 -> x0, matrix products: 26.1 us -> none  [the longest x6 12.1 us: contract_first(): lax.dot_general(left, right, (((0,), (0,)), ((), ())), preferred_element_...]
    gather x9 -> x0, local copies, waits for them, and re-layouts: 21.8 us -> none  [the longest x1 3.51 us: shards(): packed_grads = jnp.concatenate([recv_grads, zero_row], 0)[pack_order]]
    another operation x10 -> x0, local copies, waits for them, and re-layouts: 10.1 us -> none  [the longest x3 6.02 us: sum_packed(): lines = jnp.concatenate([b.reshape(devices, -1) for b in pieces], axis=1)]
    concatenate x5 -> x0, other arithmetic: 5.49 us -> none  [the longest x2 3.3 us: sent_together(): both = jnp.concatenate(arrays, axis=along)]
  transfers between devices with their start and end apart: 5 -> 0, of which waited for: 3 -> 0; matrix products, arithmetic and copies ran while one was open for 6% -> 0% of each run, Pallas kernels for 0% -> 0%
where the time goes in v1:
time: 108 us; the launch traced here: 107 us
  Pallas kernels  101 us (94%)
  local copies, waits for them, and re-layouts  5.24 us (5%)
  between operations  1.3 us (1%)
    pallas_call x1, Pallas kernels, shards(): pl.pallas_call(kernel, out_shape=(jax.ShapeDtypeStruct((rows_tok, width),...  101 us
    unnamed x16, local copies, waits for them, and re-layouts  5.24 us

profile of v1, /device:TPU:1, one launch (start us, length us, event | category | flops | bytes accessed | tf_op | source)
XLA Modules:
  0.0 107.3 jit_solution(6944912273406338862)
XLA Ops:
  1.3 100.7 %shard_map.127 = (bf16[128,1024]{1,0:T(8,128)(2,1)}, bf16[128,1024]{1,0:T(8,128)(2,1)}, f32[2,128]{1,0:T(2,128)}, bf16[1,64,384]{2,1,0:T(8,128)(2,1)}, bf16[1,64...) custom-call(bf16[128,1024]{1,0:T(8,128)(2,1)} %tok.1, bf16[128,1024]{1,0:T(8,128)(2,1)} %cot.1, s32[2,128]{1,0:T(2,128)} %bitcast.4, ...), custom_call_target="tpu_custom_call" | custom-call | flops 3623878656 | bytes 2097152 | tf_op jit(solution)/shard_map/pallas_call | solution.py:388
  102.0 0.0 copy-start
  102.0 1.7 %copy.21 = bf16[128,1024]{1,0:T(8,128)(2,1)} copy(bf16[128,1024]{1,0:T(8,128)(2,1)} %get-tuple-element.24) | data formatting | bytes 524288
  103.7 0.0 copy-done
  103.7 0.0 copy-start.4
  103.7 0.0 copy-start.3
  103.7 0.7 copy.22
  104.4 0.0 copy-done.4
  104.4 0.6 copy.23
  105.0 0.0 copy-done.3
  105.0 0.0 copy-start.2
  105.0 0.6 copy.24
  105.6 0.2 copy-done.2
  105.8 0.0 copy-start.1
  105.8 0.6 copy.25
  106.5 0.2 copy-done.1
  106.6 0.6 copy.26
Async XLA Ops:
  102.0 1.7 %copy-start = (bf16[128,1024]{1,0:T(8,128)(2,1)S(1)}, bf16[128,1024]{1,0:T(8,128)(2,1)}, u32[]{:S(2)}) copy-start(bf16[128,1024]{1,0:T(8,128)(2,1)} %get-tuple-element.25) | copy-start | bytes 786436
  103.7 0.7 copy-start.4
  103.7 1.3 %copy-start.3 = (bf16[1,64,384]{2,1,0:T(8,128)(2,1)S(1)}, bf16[1,64,384]{2,1,0:T(8,128)(2,1)}, u32[]{:S(2)}) copy-start(bf16[1,64,384]{2,1,0:T(8,128)(2,1)} %get-tuple-element.27) | copy-start | bytes 147460
  105.0 0.8 copy-start.2
  105.8 0.8 copy-start.1

commit v2 on v1

--- a/solution.py
+++ b/solution.py
@@ -51,18 +51,27 @@
     zl, c = lax.div(dp, 2), lax.rem(dp, 2)
     y, zh, x = lax.div(ex, 2 * NX), lax.rem(lax.div(ex, NX), 2), lax.rem(ex, NX)
     z = zh * NZL + zl
-    me = y * (2 * NX) + c * NX + x
+    half = NX * NY
+    spot = y * NX + x
+    me = c * half + spot
 
     def along_z(zz, core):
         return (lax.rem(zz, NZL) * 2 + core, y * (2 * NX) + lax.div(zz, NZL) * NX + x)
 
     def in_plane(q):
-        qy, qc, qx = lax.div(q, 2 * NX), lax.rem(lax.div(q, NX), 2), lax.rem(q, NX)
+        qc, qy, qx = lax.div(q, half), lax.rem(lax.div(q, NX), NY), lax.rem(q, NX)
         return (zl * 2 + qc, qy * (2 * NX) + zh * NX + qx)
 
     ring = (along_z(lax.rem(z + 1, nz), c), along_z(lax.rem(z + nz - 1, nz), c))
     other = along_z(z, 1 - c)
-    reach = (NZL, NZL - 1)
+
+    def reach(flow, h):
+        return NZL - lax.rem(h + flow, 2)
+
+    def mixed_order(o):
+        dx = lax.rem(o, NX)
+        dy = lax.rem(lax.div(o, NX) + dx, NY)
+        return lax.rem(y + dy, NY) * NX + lax.rem(x + dx, NX)
 
     def remote(src, dst, send_sem, recv_sem, device):
         return pltpu.make_async_remote_copy(
@@ -94,9 +103,9 @@
             shards_in[q].at[0], weights[q].at[dp], push_send.at[q], push_recv.at[q], other
         )
 
-    def ag_copy(q, flow, block):
-        at = weights[q].at[pl.ds(2 * block, 2)]
-        return remote(at, at, ag_send.at[flow, block, q], ag_recv.at[block, q], ring[flow])
+    def ag_copy(q, flow, block, h):
+        at = weights[q].at[2 * block + h]
+        return remote(at, at, ag_send.at[flow, block, h, q], ag_recv.at[block, h, q], ring[flow])
 
     def source(flow, hops):
         zz = lax.rem(z - hops + nz, nz) if flow == 0 else lax.rem(z + hops, nz)
@@ -111,10 +120,12 @@
     def _():
         for q in range(3):
             weights[q][dp] = shards_in[q][0]
+            for flow in (0, 1):
+                ag_copy(q, flow, zl, c).start()
         for q in range(3):
             pltpu.make_async_copy(weights[q].at[dp], weights[q].at[dp], push_recv.at[q]).wait()
             for flow in (0, 1):
-                ag_copy(q, flow, zl).start()
+                ag_copy(q, flow, zl, 1 - c).start()
 
     eye = lax.broadcasted_iota(jnp.int32, (rows_tok, rows_tok), 0) == lax.broadcasted_iota(
         jnp.int32, (rows_tok, rows_tok), 1
@@ -135,7 +146,9 @@
     slot, weight = [], []
     taken = jnp.zeros((1, planes), F32)
     for k in range(2):
-        expert = column(routing[k : k + 1, :].astype(F32))
+        named = routing[k : k + 1, :]
+        qy, qc, qx = lax.div(named, 2 * NX), lax.rem(lax.div(named, NX), 2), lax.rem(named, NX)
+        expert = column((qc * half + qy * NX + qx).astype(F32))
         weight.append(column(gates[k : k + 1, :]))
         onehot = jnp.where((expert == lanes) & alive, 1.0, 0.0)
         before = dot(earlier, onehot.astype(BF)) + taken
@@ -155,18 +168,17 @@
             remote(send_c.at[q], recv_c.at[me], a2a_send.at[1], a2a_recv.at[1], in_plane(q)),
         )
 
-    group = 2 * NX
-    for j in range(NY):
-        first = lax.rem(y + j, NY) * group
-        p0, p1 = (picks(k, first * CAP, group * CAP) for k in range(2))
-        shape = (group, CAP, width)
-        send_x[pl.ds(first, group)] = contract_first(p0 + p1, tok[...]).astype(BF).reshape(shape)
-        send_c[pl.ds(first, group)] = (
+    for j in range(2):
+        first = lax.rem(c + j, 2) * half
+        p0, p1 = (picks(k, first * CAP, half * CAP) for k in range(2))
+        shape = (half, CAP, width)
+        send_x[pl.ds(first, half)] = contract_first(p0 + p1, tok[...]).astype(BF).reshape(shape)
+        send_c[pl.ds(first, half)] = (
             (contract_first(p0, scaled[0]) + contract_first(p1, scaled[1])).astype(BF).reshape(shape)
         )
 
         def send(o, _, first=first):
-            q = first + lax.rem(x + o, group)
+            q = first + mixed_order(o)
 
             @pl.when(q != me)
             def _():
@@ -175,22 +187,24 @@
 
             return 0
 
-        lax.fori_loop(0, group, send, 0)
+        lax.fori_loop(0, half, send, 0)
     recv_x[me] = send_x[me]
     recv_c[me] = send_c[me]
 
     def forward(s, _):
-        for q in range(3):
-            for flow in (0, 1):
-                block, ours = source(flow, s)
-
-                @pl.when(ours & (s <= reach[flow]))
-                def _(q=q, flow=flow, block=block):
-                    ag_copy(q, flow, block).wait_recv()
-
-                    @pl.when(s < reach[flow])
-                    def _():
-                        ag_copy(q, flow, block).start()
+        for h in range(2):
+            for q in range(3):
+                for flow in (0, 1):
+                    block, ours = source(flow, s)
+                    far = reach(flow, h)
+
+                    @pl.when(ours & (s <= far))
+                    def _(q=q, flow=flow, h=h, block=block, far=far):
+                        ag_copy(q, flow, block, h).wait_recv()
+
+                        @pl.when(s < far)
+                        def _():
+                            ag_copy(q, flow, block, h).start()
 
         return 0
 
@@ -211,51 +225,28 @@
     per = planes // tiles
     tile_rows = per * CAP
 
-    def combine(q):
-        return (
-            remote(send_o.at[q], back_o.at[me], back_send.at[0], back_recv.at[0], in_plane(q)),
-            remote(send_p.at[q], back_p.at[me], back_send.at[1], back_recv.at[1], in_plane(q)),
-        )
-
-    def tile(t, _):
-        first = lax.rem(lax.div(y * tiles, NY) + t, tiles) * per
-        rows = pl.multiple_of(first * CAP, tile_rows)
+    def gate_up():
+        return wg[...].reshape(width, ff), wu[...].reshape(width, ff)
+
+    def inner(t, _):
+        first = t * per
+        rows = pl.ds(pl.multiple_of(first * CAP, tile_rows), tile_rows)
         xs = recv_x[pl.ds(first, per)].reshape(tile_rows, width)
         cs = recv_c[pl.ds(first, per)].reshape(tile_rows, width)
-        gate_w = wg[...].reshape(width, ff)
-        up_w = wu[...].reshape(width, ff)
-        down_w = down_full[...]
+        gate_w, up_w = gate_up()
         pre_gate = dot(xs, gate_w)
         pre_up = dot(xs, up_w)
+        hidden_grad = contract_last(cs, down_full[...])
         sig = jax.nn.sigmoid(pre_gate)
         swish = pre_gate * sig
-        hid = (swish * pre_up).astype(BF)
-        hidden[pl.ds(rows, tile_rows)] = hid
-        send_o[pl.ds(first, per)] = dot(hid, down_w).astype(BF).reshape(per, CAP, width)
-        hidden_grad = contract_last(cs, down_w)
-        gate_pre = (hidden_grad * pre_up * sig * (1.0 + pre_gate * (1.0 - sig))).astype(BF)
-        up_pre = (hidden_grad * swish).astype(BF)
-        pre_grads[pl.ds(rows, tile_rows), :ff] = gate_pre
-        pre_grads[pl.ds(rows, tile_rows), ff:] = up_pre
-        part = contract_last(gate_pre, gate_w) + contract_last(up_pre, up_w)
-        send_p[pl.ds(first, per)] = part.astype(BF).reshape(per, CAP, width)
-
-        def send(o, _):
-            q = first + lax.rem(group * (y % 2) + x + o, per)
-
-            @pl.when(q != me)
-            def _():
-                for copy in combine(q):
-                    copy.start()
-
-            return 0
-
-        lax.fori_loop(0, per, send, 0)
+        hidden[rows] = (swish * pre_up).astype(BF)
+        pre_grads[rows, :ff] = (
+            hidden_grad * pre_up * sig * (1.0 + pre_gate * (1.0 - sig))
+        ).astype(BF)
+        pre_grads[rows, ff:] = (hidden_grad * swish).astype(BF)
         return 0
 
-    lax.fori_loop(0, tiles, tile, 0)
-    back_o[me] = send_o[me]
-    back_p[me] = send_p[me]
+    lax.fori_loop(0, tiles, inner, 0)
 
     own, sums = (own_g, own_u, own_d), (sum_g, sum_u, sum_d)
     both = contract_first(recv_x[...].reshape(slots, width), pre_grads[...])
@@ -265,38 +256,77 @@
     for i in range(nz):
         own_d[i] = down_grad[i * shard_rows : (i + 1) * shard_rows].astype(BF)
 
-    def rs_copy(q, flow, block, src):
-        at = sums[q].at[flow, pl.ds(2 * block, 2)]
-        return remote(src, at, rs_send.at[flow, block, q], rs_recv.at[flow, block, q], ring[flow])
+    def rs_copy(q, flow, block, h, src):
+        at = sums[q].at[flow, 2 * block + h]
+        return remote(
+            src, at, rs_send.at[flow, block, h, q], rs_recv.at[flow, block, h, q], ring[flow]
+        )
 
     def target(flow, hops):
         return source(1 - flow, hops)
 
+    for h in range(2):
+        for q in range(3):
+            for flow in (0, 1):
+                block, ours = target(flow, reach(flow, h))
+
+                @pl.when(ours)
+                def _(q=q, flow=flow, h=h, block=block):
+                    rs_copy(q, flow, block, h, own[q].at[2 * block + h]).start()
+
+    def combine(q):
+        return (
+            remote(send_o.at[q], back_o.at[me], back_send.at[0], back_recv.at[0], in_plane(q)),
+            remote(send_p.at[q], back_p.at[me], back_send.at[1], back_recv.at[1], in_plane(q)),
+        )
+
+    def outer(t, _):
+        first = lax.rem(t + c, tiles) * per
+        rows = pl.ds(pl.multiple_of(first * CAP, tile_rows), tile_rows)
+        gate_w, up_w = gate_up()
+        shape = (per, CAP, width)
+        send_o[pl.ds(first, per)] = dot(hidden[rows], down_full[...]).astype(BF).reshape(shape)
+        part = contract_last(pre_grads[rows, :ff], gate_w)
+        part += contract_last(pre_grads[rows, ff:], up_w)
+        send_p[pl.ds(first, per)] = part.astype(BF).reshape(shape)
+
+        def send(o, _):
+            q = first + mixed_order(o)
+
+            @pl.when(q != me)
+            def _():
+                for copy in combine(q):
+                    copy.start()
+
+            return 0
+
+        lax.fori_loop(0, per, send, 0)
+        return 0
+
+    lax.fori_loop(0, tiles, outer, 0)
+    back_o[me] = send_o[me]
+    back_p[me] = send_p[me]
+
     def summing(s, _):
-        for q in range(3):
-            for flow in (0, 1):
-                left = reach[flow] - s
-                block, ours = target(flow, left)
-                here = pl.ds(2 * block, 2)
-
-                @pl.when(ours & (left > 0))
-                def _(q=q, flow=flow, block=block, here=here):
-                    @pl.when(s == 0)
-                    def _():
-                        rs_copy(q, flow, block, own[q].at[here]).start()
-
-                    @pl.when(s > 0)
-                    def _():
+        for h in range(2):
+            for q in range(3):
+                for flow in (0, 1):
+                    left = reach(flow, h) - s
+                    block, ours = target(flow, left)
+
+                    @pl.when(ours & (left > 0))
+                    def _(q=q, flow=flow, h=h, block=block):
+                        here = 2 * block + h
                         at = sums[q].at[flow, here]
-                        rs_copy(q, flow, block, at).wait_recv()
+                        rs_copy(q, flow, block, h, at).wait_recv()
                         sums[q][flow, here] = (
                             sums[q][flow, here].astype(F32) + own[q][here].astype(F32)
                         ).astype(BF)
-                        rs_copy(q, flow, block, at).start()
+                        rs_copy(q, flow, block, h, at).start()
 
         return 0
 
-    lax.fori_loop(0, NZL, summing, 0)
+    lax.fori_loop(1, NZL, summing, 0)
 
     all_of(back_o, back_recv.at[0], planes - 1)
     all_of(back_p, back_recv.at[1], planes - 1)
@@ -317,22 +347,24 @@
 
     @pl.when(zh == c)
     def _():
-        here = pl.ds(2 * zl, 2)
-        for q in range(3):
-            for flow in (0, 1):
-                at = sums[q].at[flow, here]
-                rs_copy(q, flow, zl, at).wait_recv()
-            fins[q][...] = (
-                (
-                    own[q][here].astype(F32)
-                    + sums[q][0, here].astype(F32)
-                    + sums[q][1, here].astype(F32)
-                )
-                * (1.0 / nz)
-            ).astype(BF)
-            fin_copy(q).start()
+        for h in (1 - c, c):
+            here = 2 * zl + h
+            for q in range(3):
+                for flow in (0, 1):
+                    at = sums[q].at[flow, here]
+                    rs_copy(q, flow, zl, h, at).wait_recv()
+                fins[q][h] = (
+                    (
+                        own[q][here].astype(F32)
+                        + sums[q][0, here].astype(F32)
+                        + sums[q][1, here].astype(F32)
+                    )
+                    * (1.0 / nz)
+                ).astype(BF)
+                if h is not c:
+                    fin_copy(q).start()
+        for q in range(3):
             outs[q][0] = fins[q][c]
-        for q in range(3):
             fin_copy(q).wait_send()
 
     @pl.when(zh != c)
@@ -347,19 +379,21 @@
             push(q).wait_send()
 
     def sent(s, _):
-        for q in range(3):
-            for flow in (0, 1):
-                block, ours = source(flow, s)
-
-                @pl.when(ours & (s < reach[flow]))
-                def _(q=q, flow=flow, block=block):
-                    ag_copy(q, flow, block).wait_send()
-
-                block, ours = target(flow, s + 1)
-
-                @pl.when(ours & (s < reach[flow]))
-                def _(q=q, flow=flow, block=block):
-                    rs_copy(q, flow, block, own[q].at[pl.ds(2 * block, 2)]).wait_send()
+        for h in range(2):
+            for q in range(3):
+                for flow in (0, 1):
+                    far = reach(flow, h)
+                    block, ours = source(flow, s)
+
+                    @pl.when(ours & (s < far))
+                    def _(q=q, flow=flow, h=h, block=block):
+                        ag_copy(q, flow, block, h).wait_send()
+
+                    block, ours = target(flow, s + 1)
+
+                    @pl.when(ours & (s < far))
+                    def _(q=q, flow=flow, h=h, block=block):
+                        rs_copy(q, flow, block, h, own[q].at[2 * block + h]).wait_send()
 
         return 0
 
@@ -371,6 +405,17 @@
         (send_p, back_send.at[1]),
     ):
         all_of(ref, sem, planes - 1)
+
+
+def hand_over(*refs):
+    half = len(refs) // 3
+    copies = [
+        pltpu.make_async_copy(refs[i], refs[half + i], refs[2 * half + i]) for i in range(half)
+    ]
+    for copy in copies:
+        copy.start()
+    for copy in copies:
+        copy.wait()
 
 
 def shards(
@@ -405,12 +450,12 @@
             *(pltpu.VMEM((2, nz, *s), BF) for s in shapes),
             *(pltpu.VMEM((2, *s), BF) for s in shapes),
             *(pltpu.VMEM(s, BF) for s in shapes),
-            dma((2, NZL, 3)),
-            dma((NZL, 3)),
+            dma((2, NZL, 2, 3)),
+            dma((NZL, 2, 3)),
             dma((3,)),
             dma((3,)),
-            dma((2, NZL, 3)),
-            dma((2, NZL, 3)),
+            dma((2, NZL, 2, 3)),
+            dma((2, NZL, 2, 3)),
             dma((3,)),
             dma((3,)),
             dma((2,)),
@@ -428,6 +473,14 @@
         tokens, cotangent, routing.T, gate_values.T, live_counts,
         gate_weights, up_weights, down_weights,
     )
+    hbm = pl.BlockSpec(memory_space=pl.ANY)
+    outs = pl.pallas_call(
+        hand_over,
+        out_shape=tuple(jax.ShapeDtypeStruct(o.shape, o.dtype) for o in outs),
+        in_specs=[hbm] * len(outs),
+        out_specs=tuple([hbm] * len(outs)),
+        scratch_shapes=[pltpu.SemaphoreType.DMA] * len(outs),
+    )(*outs)
     mixed, token_grad, gate_grad, grad_g, grad_u, grad_d = outs
     return mixed, token_grad, gate_grad.T, grad_g, grad_u, grad_d
 

time: 108 us -> 111 us (1.028)
  the two profiles are of different devices: /device:TPU:1 before, /device:TPU:2 now
where the time goes in v2:
time: 111 us
  Pallas kernels  110 us (99%)
  between operations  1.29 us (1%)
    pallas_call x1, Pallas kernels, shards(): pl.pallas_call(kernel, out_shape=(jax.ShapeDtypeStruct((rows_tok, width),...  88 us
    pallas_call x1, Pallas kernels, shards(): pl.pallas_call(hand_over, out_shape=tuple((jax.ShapeDtypeStruct(o.shape,...  21.5 us

profile of v2, /device:TPU:2, one launch (start us, length us, event | category | flops | bytes accessed | tf_op | source)
XLA Modules:
  0.0 110.8 jit_solution(5343901307141417263)
XLA Ops:
  1.3 88.0 %shard_map.127 = (bf16[128,1024]{1,0:T(8,128)(2,1)}, bf16[128,1024]{1,0:T(8,128)(2,1)}, f32[2,128]{1,0:T(2,128)}, bf16[1,64,384]{2,1,0:T(8,128)(2,1)}, bf16[1,64...) custom-call(bf16[128,1024]{1,0:T(8,128)(2,1)} %tok.1, bf16[128,1024]{1,0:T(8,128)(2,1)} %cot.1, s32[2,128]{1,0:T(2,128)} %bitcast.3, ...), custom_call_target="tpu_custom_call" | custom-call | flops 3623878656 | bytes 2097152 | tf_op jit(solution)/shard_map/pallas_call | solution.py:433
  89.3 21.5 %shard_map.128 = (bf16[128,1024]{1,0:T(8,128)(2,1)}, bf16[128,1024]{1,0:T(8,128)(2,1)}, f32[2,128]{1,0:T(2,128)}, bf16[1,64,384]{2,1,0:T(8,128)(2,1)}, bf16[1,64...) custom-call(bf16[128,1024]{1,0:T(8,128)(2,1)} %get-tuple-element.18.refs_0_, ...), custom_call_target="tpu_custom_call" | custom-call | tf_op jit(solution)/shard_map/pallas_call | solution.py:477

commit v3 on v2

v3 whole, which is shorter than its diff:
```python
import functools

import jax
import jax.numpy as jnp
from jax import lax
from jax.experimental import pallas as pl
from jax.experimental.pallas import tpu as pltpu
from jax.sharding import PartitionSpec as P

NX, NY, NZL = 4, 4, 8
CAP = 16
BF, F32 = jnp.bfloat16, jnp.float32


def contract_last(left, right):
    return lax.dot_general(
        left, right, (((1,), (1,)), ((), ())), preferred_element_type=F32
    )


def contract_first(left, right):
    return lax.dot_general(
        left, right, (((0,), (0,)), ((), ())), preferred_element_type=F32
    )


def dot(left, right):
    return jnp.dot(left, right, preferred_element_type=F32)


def kernel(
    tok, cot, routing, gates, live,
    gate_in, up_in, down_in,
    mixed, token_grad, gate_grad, out_g, out_u, out_d,
    all_g, all_u, all_d, down_full,
    send_rows, recv_rows, send_back, recv_back,
    hidden, pre_grads,
    part_g, part_u, part_d, sum_g, sum_u, sum_d,
    ag_send, ag_recv, pass_send, pass_recv,
    rs_send, rs_recv, push_send, push_recv,
    a2a_send, a2a_recv, back_send, back_recv,
):
    rows_tok, width = tok.shape
    planes = 2 * NX * NY
    nz = 2 * NZL
    slots = planes * CAP
    ff = gate_in.shape[-1]

    dp, ex = lax.axis_index("dp"), lax.axis_index("expert")
    zl, c = lax.div(dp, 2), lax.rem(dp, 2)
    y, zh, x = lax.div(ex, 2 * NX), lax.rem(lax.div(ex, NX), 2), lax.rem(ex, NX)
    z = zh * NZL + zl
    half = NX * NY
    spot = y * NX + x
    me = c * half + spot

    def along_z(zz, core):
        return (lax.rem(zz, NZL) * 2 + core, y * (2 * NX) + lax.div(zz, NZL) * NX + x)

    def in_plane(q):
        qc, qy, qx = lax.div(q, half), lax.rem(lax.div(q, NX), NY), lax.rem(q, NX)
        return (zl * 2 + qc, qy * (2 * NX) + zh * NX + qx)

    ring = (along_z(lax.rem(z + 1, nz), c), along_z(lax.rem(z + nz - 1, nz), c))
    other = along_z(z, 1 - c)

    def far(flow, core):
        return NZL - lax.rem(core + flow, 2)

    def source(flow, hops):
        return lax.rem(z - hops + nz, nz) if flow == 0 else lax.rem(z + hops, nz)

    def target(flow, hops):
        return source(1 - flow, hops)

    def family(zz):
        return lax.div(zz, NZL)

    def mixed_order(o):
        dx = lax.rem(o, NX)
        dy = lax.rem(lax.div(o, NX) + dx, NY)
        return lax.rem(y + dy, NY) * NX + lax.rem(x + dx, NX)

    def remote(src, dst, send_sem, recv_sem, device):
        return pltpu.make_async_remote_copy(
            src_ref=src, dst_ref=dst, send_sem=send_sem, recv_sem=recv_sem,
            device_id=device, device_id_type=pl.DeviceIdType.MESH,
        )

    barrier = pltpu.get_barrier_semaphore()

    def greet(o, _):
        pl.semaphore_signal(
            barrier, inc=1, device_id=in_plane(lax.rem(me + o, planes)),
            device_id_type=pl.DeviceIdType.MESH,
        )
        return 0

    for device in ring:
        pl.semaphore_signal(
            barrier, inc=1, device_id=device, device_id_type=pl.DeviceIdType.MESH
        )
    lax.fori_loop(1, planes, greet, 0)
    pl.semaphore_wait(barrier, planes + 1)

    shards_in, gathered = (gate_in, up_in, down_in), (all_g, all_u, all_d)
    first_own = c * nz

    def ag_copy(q, flow, zz):
        at = gathered[q].at[2 * zz + c]
        return remote(at, at, ag_send.at[flow, zz, q], ag_recv.at[zz, q], ring[flow])

    def pass_copy(q, zz):
        at = gathered[q].at[2 * zz + c]
        return remote(
            at, at, pass_send.at[lax.rem(zz, NZL), q], pass_recv.at[lax.rem(zz, NZL), q], other
        )

    def pass_on(q, zz):
        @pl.when(family(zz) != c)
        def _():
            pass_copy(q, zz).start()

    for q in range(3):
        gathered[q][2 * z + c] = shards_in[q][0]
        for flow in (0, 1):
            ag_copy(q, flow, z).start()
        pass_on(q, z)

    def forward(s):
        for q in range(3):
            for flow in (0, 1):
                zz = source(flow, s)

                def arrived(q=q, flow=flow, zz=zz):
                    ag_copy(q, flow, zz).wait_recv()

                def onward(q=q, flow=flow, zz=zz):
                    ag_copy(q, flow, zz).start()

                if s < NZL - 1:
                    arrived()
                    onward()
                    pass_on(q, zz)
                elif s == NZL - 1:
                    arrived()
                    pl.when(far(flow, c) == NZL)(onward)
                    pass_on(q, zz)
                else:

                    @pl.when(far(flow, c) == NZL)
                    def _(q=q, zz=zz, arrived=arrived):
                        arrived()
                        pass_on(q, zz)

    eye = lax.broadcasted_iota(jnp.int32, (rows_tok, rows_tok), 0) == lax.broadcasted_iota(
        jnp.int32, (rows_tok, rows_tok), 1
    )

    def column(row):
        return jnp.sum(jnp.where(eye, row, 0.0), axis=1, keepdims=True)

    def row_of(col):
        return jnp.sum(jnp.where(eye, col, 0.0), axis=0, keepdims=True)

    alive = lax.broadcasted_iota(jnp.int32, (rows_tok, 1), 0) < live[0]
    lanes = lax.broadcasted_iota(jnp.int32, (rows_tok, planes), 1).astype(F32)
    earlier = (
        lax.broadcasted_iota(jnp.int32, (rows_tok, rows_tok), 1)
        < lax.broadcasted_iota(jnp.int32, (rows_tok, rows_tok), 0)
    ).astype(BF)
    slot, weight = [], []
    taken = jnp.zeros((1, planes), F32)
    for k in range(2):
        named = routing[k : k + 1, :]
        qy, qc, qx = lax.div(named, 2 * NX), lax.rem(lax.div(named, NX), 2), lax.rem(named, NX)
        expert = column((qc * half + qy * NX + qx).astype(F32))
        weight.append(column(gates[k : k + 1, :]))
        onehot = jnp.where((expert == lanes) & alive, 1.0, 0.0)
        before = dot(earlier, onehot.astype(BF)) + taken
        taken = taken + jnp.sum(onehot, axis=0, keepdims=True)
        found = jnp.sum(onehot * (before + lanes * CAP), axis=1, keepdims=True)
        slot.append(jnp.where(alive, found, -1.0).astype(jnp.int32))

    def picks(k, start, count):
        at = lax.broadcasted_iota(jnp.int32, (rows_tok, count), 1) + start
        return jnp.where(slot[k] == at, 1.0, 0.0).astype(BF)

    scaled = [(weight[k] * cot[...].astype(F32)).astype(BF) for k in range(2)]

    def dispatch(q):
        return remote(send_rows.at[q], recv_rows.at[me], a2a_send, a2a_recv, in_plane(q))

    for j in range(2):
        first = lax.rem(c + j, 2) * half
        p0, p1 = (picks(k, first * CAP, half * CAP) for k in range(2))
        shape = (half, CAP, width)
        send_rows[pl.ds(first, half), 0] = contract_first(p0 + p1, tok[...]).astype(BF).reshape(shape)
        send_rows[pl.ds(first, half), 1] = (
            (contract_first(p0, scaled[0]) + contract_first(p1, scaled[1])).astype(BF).reshape(shape)
        )

        def send(o, _, first=first):
            q = first + mixed_order(o)

            @pl.when(q != me)
            def _():
                dispatch(q).start()

            return 0

        lax.fori_loop(0, half, send, 0)
        if j + 1 <= NZL:
            forward(j + 1)
    recv_rows[me] = send_rows[me]

    for s in range(3, NZL + 1):
        forward(s)

    def passed(b, _):
        for q in range(3):
            at = gathered[q].at[first_own + 2 * b + 1 - c]
            pltpu.make_async_copy(at, at, pass_recv.at[b, q]).wait()
        return 0

    lax.fori_loop(0, NZL, passed, 0)

    shard_rows = down_in.shape[1]
    for i in range(nz):
        down_full[i * shard_rows : (i + 1) * shard_rows] = all_d[first_own + i]

    def all_of(ref, sem, count):
        part = ref.at[pl.ds(0, count)]
        pltpu.make_async_copy(part, part, sem).wait()

    all_of(recv_rows, a2a_recv, planes - 1)

    tiles = 2
    per = planes // tiles
    tile_rows = per * CAP

    def gate_up():
        mine = pl.ds(first_own, nz)
        return all_g[mine].reshape(width, ff), all_u[mine].reshape(width, ff)

    def inner(t, _):
        first = t * per
        rows = pl.ds(pl.multiple_of(first * CAP, tile_rows), tile_rows)
        xs = recv_rows[pl.ds(first, per), 0].reshape(tile_rows, width)
        cs = recv_rows[pl.ds(first, per), 1].reshape(tile_rows, width)
        gate_w, up_w = gate_up()
        pre_gate = dot(xs, gate_w)
        pre_up = dot(xs, up_w)
        hidden_grad = contract_last(cs, down_full[...])
        sig = jax.nn.sigmoid(pre_gate)
        swish = pre_gate * sig
        hidden[rows] = (swish * pre_up).astype(BF)
        pre_grads[rows, :ff] = (
            hidden_grad * pre_up * sig * (1.0 + pre_gate * (1.0 - sig))
        ).astype(BF)
        pre_grads[rows, ff:] = (hidden_grad * swish).astype(BF)
        return 0

    lax.fori_loop(0, tiles, inner, 0)

    parts, sums = (part_g, part_u, part_d), (sum_g, sum_u, sum_d)
    mine = pl.ds(first_own, nz)
    both = contract_first(recv_rows[:, 0].reshape(slots, width), pre_grads[...])
    shape = (nz, width // nz, ff)
    part_g[mine] = both[:, :ff].astype(BF).reshape(shape)
    part_u[mine] = both[:, ff:].astype(BF).reshape(shape)
    down_grad = contract_first(hidden[...], recv_rows[:, 1].reshape(slots, width))
    for i in range(nz):
        part_d[first_own + i] = down_grad[i * shard_rows : (i + 1) * shard_rows].astype(BF)

    def push_copy(q, zz):
        at, b = parts[q].at[2 * zz + 1 - c], lax.rem(zz, NZL)
        return remote(at, at, push_send.at[b, q], push_recv.at[b, q], other)

    def pushed(q, zz):
        @pl.when(family(zz) != c)
        def _():
            at = parts[q].at[2 * zz + c]
            pltpu.make_async_copy(at, at, push_recv.at[lax.rem(zz, NZL), q]).wait()

    def push(s, _):
        for q in range(3):
            for flow in (0, 1):
                left = far(flow, 1 - c) - s
                zz = target(flow, left)

                @pl.when((family(zz) == c) & (left > 0))
                def _(q=q, zz=zz):
                    push_copy(q, zz).start()

        return 0

    lax.fori_loop(0, NZL, push, 0)
    for q in range(3):

        @pl.when(zh == c)
        def _(q=q):
            push_copy(q, z).start()

    def rs_copy(q, flow, zz, src):
        return remote(
            src, sums[q].at[flow, zz], rs_send.at[flow, zz, q], rs_recv.at[flow, zz, q], ring[flow]
        )

    def summing(left):
        for q in range(3):
            for flow in (0, 1):
                zz = target(flow, left)

                def begin(q=q, flow=flow, zz=zz):
                    pushed(q, zz)
                    rs_copy(q, flow, zz, parts[q].at[2 * zz + c]).start()

                def add(q=q, flow=flow, zz=zz):
                    at = sums[q].at[flow, zz]
                    pushed(q, zz)
                    rs_copy(q, flow, zz, at).wait_recv()
                    sums[q][flow, zz] = (
                        sums[q][flow, zz].astype(F32) + parts[q][2 * zz + c].astype(F32)
                    ).astype(BF)
                    rs_copy(q, flow, zz, at).start()

                farthest = far(flow, c) == NZL
                if left == NZL:
                    pl.when(farthest)(begin)
                elif left == NZL - 1:
                    pl.when(jnp.logical_not(farthest))(begin)
                    pl.when(farthest)(add)
                else:
                    add()

    summing(NZL)

    def combine(q):
        return remote(send_back.at[q], recv_back.at[me], back_send, back_recv, in_plane(q))

    def outer(t, _):
        first = lax.rem(t + c, tiles) * per
        rows = pl.ds(pl.multiple_of(first * CAP, tile_rows), tile_rows)
        gate_w, up_w = gate_up()
        shape = (per, CAP, width)
        send_back[pl.ds(first, per), 0] = dot(hidden[rows], down_full[...]).astype(BF).reshape(shape)
        part = contract_last(pre_grads[rows, :ff], gate_w)
        part += contract_last(pre_grads[rows, ff:], up_w)
        send_back[pl.ds(first, per), 1] = part.astype(BF).reshape(shape)

        def send(o, _):
            q = first + mixed_order(o)

            @pl.when(q != me)
            def _():
                combine(q).start()

            return 0

        lax.fori_loop(0, per, send, 0)
        return 0

    lax.fori_loop(0, tiles, outer, 0)
    recv_back[me] = send_back[me]
    for left in range(NZL - 1, 0, -1):
        summing(left)

    all_of(recv_back, back_recv, planes - 1)
    p0, p1 = (picks(k, 0, slots) for k in range(2))
    token_grad[...] = dot(p0 + p1, recv_back[:, 1].reshape(slots, width)).astype(BF)
    total = jnp.zeros((rows_tok, width), F32)
    cot_f = cot[...].astype(F32)
    for k, p in enumerate((p0, p1)):
        got = dot(p, recv_back[:, 0].reshape(slots, width))
        total += weight[k] * got
        gate_grad[k : k + 1, :] = row_of(jnp.sum(cot_f * got, axis=1, keepdims=True))
    mixed[...] = total.astype(BF)

    outs = (out_g, out_u, out_d)
    for q in range(3):
        pushed(q, z)
        total = parts[q][2 * z + c].astype(F32)
        for flow in (0, 1):
            rs_copy(q, flow, z, sums[q].at[flow, z]).wait_recv()
            total += sums[q][flow, z].astype(F32)
        outs[q][0] = (total * (1.0 / nz)).astype(BF)

    def sent(s, _):
        for q in range(3):
            for flow in (0, 1):

                @pl.when(s < far(flow, c))
                def _(q=q, flow=flow):
                    ag_copy(q, flow, source(flow, s)).wait_send()
                    zz = target(flow, s + 1)
                    rs_copy(q, flow, zz, parts[q].at[2 * zz + c]).wait_send()

            pass_copy(q, (1 - c) * NZL + s).wait_send()
            push_copy(q, c * NZL + s).wait_send()
        return 0

    lax.fori_loop(0, NZL, sent, 0)
    all_of(send_rows, a2a_send, planes - 1)
    all_of(send_back, back_send, planes - 1)


def hand_over(*refs):
    half = len(refs) // 2
    for i in range(half):
        refs[half + i][...] = refs[i][...]


def shards(
    tokens, cotangent, routing, gate_values, live_counts, gate_weights, up_weights, down_weights
):
    rows_tok, width = tokens.shape
    ff = gate_weights.shape[-1]
    planes, nz = 2 * NX * NY, 2 * NZL
    slots = planes * CAP
    shapes = [gate_weights.shape[1:], up_weights.shape[1:], down_weights.shape[1:]]
    vmem = pl.BlockSpec(memory_space=pltpu.VMEM)
    dma = pltpu.SemaphoreType.DMA
    block = pltpu.VMEM((planes, 2, CAP, width), BF)
    flops = 18 * slots * width * ff
    outs = pl.pallas_call(
        kernel,
        out_shape=(
            jax.ShapeDtypeStruct((rows_tok, width), BF),
            jax.ShapeDtypeStruct((rows_tok, width), BF),
            jax.ShapeDtypeStruct((2, rows_tok), F32),
            *(jax.ShapeDtypeStruct((1, *s), BF) for s in shapes),
        ),
        in_specs=[vmem] * 4 + [pl.BlockSpec(memory_space=pltpu.SMEM)] + [vmem] * 3,
        out_specs=tuple([vmem] * 6),
        scratch_shapes=[
            *(pltpu.VMEM((2 * nz, *s), BF) for s in shapes),
            pltpu.VMEM((ff, width), BF),
            *([block] * 4),
            pltpu.VMEM((slots, ff), BF),
            pltpu.VMEM((slots, 2 * ff), BF),
            *(pltpu.VMEM((2 * nz, *s), BF) for s in shapes),
            *(pltpu.VMEM((2, nz, *s), BF) for s in shapes),
            dma((2, nz, 3)),
            dma((nz, 3)),
            dma((NZL, 3)),
            dma((NZL, 3)),
            dma((2, nz, 3)),
            dma((2, nz, 3)),
            dma((NZL, 3)),
            dma((NZL, 3)),
            dma,
            dma,
            dma,
            dma,
        ],
        compiler_params=pltpu.CompilerParams(
            collective_id=0, has_side_effects=True, vmem_limit_bytes=56 * 1024 * 1024
        ),
        cost_estimate=pl.CostEstimate(
            flops=flops, bytes_accessed=2 * 1024 * 1024, transcendentals=slots * ff
        ),
    )(
        tokens, cotangent, routing.T, gate_values.T, live_counts,
        gate_weights, up_weights, down_weights,
    )
    outs = pl.pallas_call(
        hand_over,
        out_shape=tuple(jax.ShapeDtypeStruct(o.shape, o.dtype) for o in outs),
        in_specs=[vmem] * len(outs),
        out_specs=tuple([vmem] * len(outs)),
    )(*outs)
    mixed, token_grad, gate_grad, grad_g, grad_u, grad_d = outs
    return mixed, token_grad, gate_grad.T, grad_g, grad_u, grad_d


def solution(mesh):
    return jax.shard_map(
        shards,
        mesh=mesh,
        in_specs=(
            P(("dp", "expert"), None),
            P(("dp", "expert"), None),
            P(("dp", "expert"), None),
            P(("dp", "expert"), None),
            P(("dp", "expert")),
            P("expert", "dp", None),
            P("expert", "dp", None),
            P("expert", "dp", None),
        ),
        out_specs=(
            P(("dp", "expert"), None),
            P(("dp", "expert"), None),
            P(("dp", "expert"), None),
            P("expert", "dp", None),
            P("expert", "dp", None),
            P("expert", "dp", None),
        ),
        check_vma=False,
    )
```

time: 111 us -> 89.8 us (0.81)
  the two profiles are of different devices: /device:TPU:2 before, /device:TPU:1 now
where the time goes in v3:
time: 89.8 us; the launch traced here: 89.6 us
  Pallas kernels  88.4 us (98%)
  between operations  1.29 us (1%)
    pallas_call x1, Pallas kernels, shards(): pl.pallas_call(kernel, out_shape=(jax.ShapeDtypeStruct((rows_tok, width),...  86.4 us
    pallas_call x1, Pallas kernels, shards(): pl.pallas_call(hand_over, out_shape=tuple((jax.ShapeDtypeStruct(o.shape,...  1.92 us

profile of v3, /device:TPU:1, one launch (start us, length us, event | category | flops | bytes accessed | tf_op | source)
XLA Modules:
  0.0 89.6 jit_solution(13899133998349254428)
XLA Ops:
  1.3 86.4 %shard_map.127 = (bf16[128,1024]{1,0:T(8,128)(2,1)}, bf16[128,1024]{1,0:T(8,128)(2,1)}, f32[2,128]{1,0:T(2,128)}, bf16[1,64,384]{2,1,0:T(8,128)(2,1)}, bf16[1,64...) custom-call(bf16[128,1024]{1,0:T(8,128)(2,1)} %tok.1, bf16[128,1024]{1,0:T(8,128)(2,1)} %cot.1, s32[2,128]{1,0:T(2,128)} %bitcast.3, ...), custom_call_target="tpu_custom_call" | custom-call | flops 3623878656 | bytes 2097152 | tf_op jit(solution)/shard_map/pallas_call | solution.py:426
  87.7 1.9 %shard_map.128 = (bf16[128,1024]{1,0:T(8,128)(2,1)}, bf16[128,1024]{1,0:T(8,128)(2,1)}, f32[2,128]{1,0:T(2,128)}, bf16[1,64,384]{2,1,0:T(8,128)(2,1)}, bf16[1,64...) custom-call(bf16[128,1024]{1,0:T(8,128)(2,1)} %get-tuple-element.18.refs_0_, ...), custom_call_target="tpu_custom_call" | custom-call | tf_op jit(solution)/shard_map/pallas_call | solution.py:467

commit v4 on v3

--- a/solution.py
+++ b/solution.py
@@ -29,15 +29,15 @@
 
 
 def kernel(
-    tok, cot, routing, gates, live,
+    tok_in, cot_in, routing, gates, live,
     gate_in, up_in, down_in,
     mixed, token_grad, gate_grad, out_g, out_u, out_d,
-    all_g, all_u, all_d, down_full,
+    tok, cot, all_g, all_u, all_d, down_full,
     send_rows, recv_rows, send_back, recv_back,
     hidden, pre_grads,
     part_g, part_u, part_d, sum_g, sum_u, sum_d,
-    ag_send, ag_recv, pass_send, pass_recv,
-    rs_send, rs_recv, push_send, push_recv,
+    load_rows, load_shards, ag_send, arrival, pass_send,
+    rs_send, rs_recv, rs_first, push_send, push_recv,
     a2a_send, a2a_recv, back_send, back_recv,
 ):
     rows_tok, width = tok.shape
@@ -61,7 +61,8 @@
         qc, qy, qx = lax.div(q, half), lax.rem(lax.div(q, NX), NY), lax.rem(q, NX)
         return (zl * 2 + qc, qy * (2 * NX) + zh * NX + qx)
 
-    ring = (along_z(lax.rem(z + 1, nz), c), along_z(lax.rem(z + nz - 1, nz), c))
+    beside = (lax.rem(z + 1, nz), lax.rem(z + nz - 1, nz))
+    ring = tuple(along_z(zz, c) for zz in beside)
     other = along_z(z, 1 - c)
 
     def far(flow, core):
@@ -87,6 +88,18 @@
             device_id=device, device_id_type=pl.DeviceIdType.MESH,
         )
 
+    shards_in, gathered = (gate_in, up_in, down_in), (all_g, all_u, all_d)
+    load = [
+        pltpu.make_async_copy(shards_in[q].at[0], gathered[q].at[2 * z + c], load_shards.at[q])
+        for q in range(3)
+    ]
+    load += [
+        pltpu.make_async_copy(tok_in, tok, load_rows.at[0]),
+        pltpu.make_async_copy(cot_in, cot, load_rows.at[1]),
+    ]
+    for copy in load:
+        copy.start()
+
     barrier = pltpu.get_barrier_semaphore()
 
     def greet(o, _):
@@ -96,36 +109,38 @@
         )
         return 0
 
-    for device in ring:
+    for device in (*ring, *(along_z(zz, 1 - c) for zz in beside)):
         pl.semaphore_signal(
             barrier, inc=1, device_id=device, device_id_type=pl.DeviceIdType.MESH
         )
     lax.fori_loop(1, planes, greet, 0)
-    pl.semaphore_wait(barrier, planes + 1)
-
-    shards_in, gathered = (gate_in, up_in, down_in), (all_g, all_u, all_d)
+    pl.semaphore_wait(barrier, planes + 3)
+
     first_own = c * nz
 
-    def ag_copy(q, flow, zz):
+    def ag_copy(q, flow, zz, core):
         at = gathered[q].at[2 * zz + c]
-        return remote(at, at, ag_send.at[flow, zz, q], ag_recv.at[zz, q], ring[flow])
+        return remote(
+            at, at, ag_send.at[flow, zz, q], arrival.at[2 * zz + c, q], along_z(beside[flow], core)
+        )
 
     def pass_copy(q, zz):
         at = gathered[q].at[2 * zz + c]
         return remote(
-            at, at, pass_send.at[lax.rem(zz, NZL), q], pass_recv.at[lax.rem(zz, NZL), q], other
-        )
-
-    def pass_on(q, zz):
-        @pl.when(family(zz) != c)
-        def _():
-            pass_copy(q, zz).start()
-
-    for q in range(3):
-        gathered[q][2 * z + c] = shards_in[q][0]
-        for flow in (0, 1):
-            ag_copy(q, flow, z).start()
-        pass_on(q, z)
+            at, at, pass_send.at[lax.rem(zz, NZL), q], arrival.at[2 * zz + c, q], other
+        )
+
+    def onward(q, flow, s, zz):
+        if s + 1 < NZL - 1:
+            ag_copy(q, flow, zz, c).start()
+        elif s + 1 == NZL - 1:
+            last = far(flow, c) == NZL - 1
+            ag_copy(q, flow, zz, jnp.where(last, family(zz), c)).start()
+        else:
+
+            @pl.when(far(flow, c) == NZL)
+            def _():
+                ag_copy(q, flow, zz, family(zz)).start()
 
     def forward(s):
         for q in range(3):
@@ -133,25 +148,38 @@
                 zz = source(flow, s)
 
                 def arrived(q=q, flow=flow, zz=zz):
-                    ag_copy(q, flow, zz).wait_recv()
-
-                def onward(q=q, flow=flow, zz=zz):
-                    ag_copy(q, flow, zz).start()
+                    ag_copy(q, flow, zz, c).wait_recv()
+
+                def pass_on(q=q, zz=zz):
+                    @pl.when(family(zz) != c)
+                    def _():
+                        pass_copy(q, zz).start()
 
                 if s < NZL - 1:
                     arrived()
-                    onward()
-                    pass_on(q, zz)
+                    onward(q, flow, s, zz)
+                    pass_on()
                 elif s == NZL - 1:
-                    arrived()
-                    pl.when(far(flow, c) == NZL)(onward)
-                    pass_on(q, zz)
+                    ends = far(flow, c) == s
+
+                    @pl.when(jnp.logical_not(ends))
+                    def _(q=q, flow=flow, zz=zz, arrived=arrived, pass_on=pass_on):
+                        arrived()
+                        onward(q, flow, s, zz)
+                        pass_on()
+
+                    pl.when(ends & (family(zz) == c))(arrived)
                 else:
-
-                    @pl.when(far(flow, c) == NZL)
-                    def _(q=q, zz=zz, arrived=arrived):
-                        arrived()
-                        pass_on(q, zz)
+                    pl.when((far(flow, c) == s) & (family(zz) == c))(arrived)
+
+    for q in range(3):
+        load[q].wait()
+        for flow in (0, 1):
+            onward(q, flow, 0, z)
+
+        @pl.when(zh != c)
+        def _(q=q):
+            pass_copy(q, z).start()
 
     eye = lax.broadcasted_iota(jnp.int32, (rows_tok, rows_tok), 0) == lax.broadcasted_iota(
         jnp.int32, (rows_tok, rows_tok), 1
@@ -186,6 +214,8 @@
         at = lax.broadcasted_iota(jnp.int32, (rows_tok, count), 1) + start
         return jnp.where(slot[k] == at, 1.0, 0.0).astype(BF)
 
+    load[3].wait()
+    load[4].wait()
     scaled = [(weight[k] * cot[...].astype(F32)).astype(BF) for k in range(2)]
 
     def dispatch(q):
@@ -219,8 +249,9 @@
 
     def passed(b, _):
         for q in range(3):
-            at = gathered[q].at[first_own + 2 * b + 1 - c]
-            pltpu.make_async_copy(at, at, pass_recv.at[b, q]).wait()
+            place = first_own + 2 * b + 1 - c
+            at = gathered[q].at[place]
+            pltpu.make_async_copy(at, at, arrival.at[place, q]).wait()
         return 0
 
     lax.fori_loop(0, NZL, passed, 0)
@@ -283,24 +314,40 @@
             at = parts[q].at[2 * zz + c]
             pltpu.make_async_copy(at, at, push_recv.at[lax.rem(zz, NZL), q]).wait()
 
-    def push(s, _):
-        for q in range(3):
-            for flow in (0, 1):
-                left = far(flow, 1 - c) - s
-                zz = target(flow, left)
-
-                @pl.when((family(zz) == c) & (left > 0))
-                def _(q=q, zz=zz):
-                    push_copy(q, zz).start()
-
-        return 0
-
-    lax.fori_loop(0, NZL, push, 0)
+    def first_copy(q, flow, h, core):
+        zz = target(flow, far(flow, core))
+        return family(zz) == c, remote(
+            parts[q].at[2 * zz + core], sums[q].at[flow, zz], rs_first.at[flow, h, q],
+            rs_recv.at[flow, zz, q], along_z(beside[flow], core),
+        )
+
     for q in range(3):
+        for flow in (0, 1):
+            for h, core in enumerate((c, 1 - c)):
+                ours, copy = first_copy(q, flow, h, core)
+                pl.when(ours)(copy.start)
+
+    def each_push(do):
+        def some(s, _):
+            for q in range(3):
+                for flow in (0, 1):
+                    left = far(flow, 1 - c) - s
+                    zz = target(flow, left)
+
+                    @pl.when((family(zz) == c) & (left > 0))
+                    def _(q=q, zz=zz):
+                        do(push_copy(q, zz))
+
+            return 0
+
+        lax.fori_loop(1, NZL, some, 0)
 
         @pl.when(zh == c)
-        def _(q=q):
-            push_copy(q, z).start()
+        def _():
+            for q in range(3):
+                do(push_copy(q, z))
+
+    each_push(lambda copy: copy.start())
 
     def rs_copy(q, flow, zz, src):
         return remote(
@@ -311,10 +358,6 @@
         for q in range(3):
             for flow in (0, 1):
                 zz = target(flow, left)
-
-                def begin(q=q, flow=flow, zz=zz):
-                    pushed(q, zz)
-                    rs_copy(q, flow, zz, parts[q].at[2 * zz + c]).start()
 
                 def add(q=q, flow=flow, zz=zz):
                     at = sums[q].at[flow, zz]
@@ -326,15 +369,10 @@
                     rs_copy(q, flow, zz, at).start()
 
                 farthest = far(flow, c) == NZL
-                if left == NZL:
-                    pl.when(farthest)(begin)
-                elif left == NZL - 1:
-                    pl.when(jnp.logical_not(farthest))(begin)
+                if left == NZL - 1:
                     pl.when(farthest)(add)
                 else:
                     add()
-
-    summing(NZL)
 
     def combine(q):
         return remote(send_back.at[q], recv_back.at[me], back_send, back_recv, in_plane(q))
@@ -389,18 +427,31 @@
     def sent(s, _):
         for q in range(3):
             for flow in (0, 1):
+                zz = source(flow, s)
 
                 @pl.when(s < far(flow, c))
-                def _(q=q, flow=flow):
-                    ag_copy(q, flow, source(flow, s)).wait_send()
-                    zz = target(flow, s + 1)
-                    rs_copy(q, flow, zz, parts[q].at[2 * zz + c]).wait_send()
-
-            pass_copy(q, (1 - c) * NZL + s).wait_send()
-            push_copy(q, c * NZL + s).wait_send()
+                def _(q=q, flow=flow, zz=zz):
+                    ag_copy(q, flow, zz, c).wait_send()
+
+                    @pl.when((family(zz) != c) & ((s > 0) | (flow == 0)))
+                    def _():
+                        pass_copy(q, zz).wait_send()
+
+                zz = target(flow, s + 1)
+
+                @pl.when(s + 1 < far(flow, c))
+                def _(q=q, flow=flow, zz=zz):
+                    rs_copy(q, flow, zz, sums[q].at[flow, zz]).wait_send()
+
         return 0
 
     lax.fori_loop(0, NZL, sent, 0)
+    each_push(lambda copy: copy.wait_send())
+    for q in range(3):
+        for flow in (0, 1):
+            for h, core in enumerate((c, 1 - c)):
+                ours, copy = first_copy(q, flow, h, core)
+                pl.when(ours)(copy.wait_send)
     all_of(send_rows, a2a_send, planes - 1)
     all_of(send_back, back_send, planes - 1)
 
@@ -420,6 +471,7 @@
     slots = planes * CAP
     shapes = [gate_weights.shape[1:], up_weights.shape[1:], down_weights.shape[1:]]
     vmem = pl.BlockSpec(memory_space=pltpu.VMEM)
+    hbm = pl.BlockSpec(memory_space=pl.ANY)
     dma = pltpu.SemaphoreType.DMA
     block = pltpu.VMEM((planes, 2, CAP, width), BF)
     flops = 18 * slots * width * ff
@@ -431,9 +483,10 @@
             jax.ShapeDtypeStruct((2, rows_tok), F32),
             *(jax.ShapeDtypeStruct((1, *s), BF) for s in shapes),
         ),
-        in_specs=[vmem] * 4 + [pl.BlockSpec(memory_space=pltpu.SMEM)] + [vmem] * 3,
+        in_specs=[hbm] * 2 + [vmem] * 2 + [pl.BlockSpec(memory_space=pltpu.SMEM)] + [hbm] * 3,
         out_specs=tuple([vmem] * 6),
         scratch_shapes=[
+            *([pltpu.VMEM((rows_tok, width), BF)] * 2),
             *(pltpu.VMEM((2 * nz, *s), BF) for s in shapes),
             pltpu.VMEM((ff, width), BF),
             *([block] * 4),
@@ -441,12 +494,14 @@
             pltpu.VMEM((slots, 2 * ff), BF),
             *(pltpu.VMEM((2 * nz, *s), BF) for s in shapes),
             *(pltpu.VMEM((2, nz, *s), BF) for s in shapes),
+            dma((2,)),
+            dma((3,)),
             dma((2, nz, 3)),
-            dma((nz, 3)),
-            dma((NZL, 3)),
+            dma((2 * nz, 3)),
             dma((NZL, 3)),
             dma((2, nz, 3)),
             dma((2, nz, 3)),
+            dma((2, 2, 3)),
             dma((NZL, 3)),
             dma((NZL, 3)),
             dma,

time: 89.8 us -> 88.4 us (0.984)
  the two profiles are of different devices: /device:TPU:1 before, /device:TPU:2 now
where the time goes in v4:
time: 88.4 us; the launch traced here: 88.2 us
  Pallas kernels  86.9 us (98%)
  between operations  1.29 us (1%)
    pallas_call x1, Pallas kernels, shards(): pl.pallas_call(kernel, out_shape=(jax.ShapeDtypeStruct((rows_tok, width),...  85 us
    pallas_call x1, Pallas kernels, shards(): pl.pallas_call(hand_over, out_shape=tuple((jax.ShapeDtypeStruct(o.shape,...  1.92 us

profile of v4, /device:TPU:2, one launch (start us, length us, event | category | flops | bytes accessed | tf_op | source)
XLA Modules:
  0.0 88.2 jit_solution(11137945679716999155)
XLA Ops:
  1.3 85.0 %shard_map.127 = (bf16[128,1024]{1,0:T(8,128)(2,1)}, bf16[128,1024]{1,0:T(8,128)(2,1)}, f32[2,128]{1,0:T(2,128)}, bf16[1,64,384]{2,1,0:T(8,128)(2,1)}, bf16[1,64...) custom-call(bf16[128,1024]{1,0:T(8,128)(2,1)} %tok_in.1, bf16[128,1024]{1,0:T(8,128)(2,1)} %cot_in.1, s32[2,128]{1,0:T(2,128)} %bitcast.3, ...), custom_call_target="tpu_custom_call" | custom-call | flops 3623878656 | bytes 2097152 | tf_op jit(solution)/shard_map/pallas_call | solution.py:478
  86.3 1.9 %shard_map.128 = (bf16[128,1024]{1,0:T(8,128)(2,1)}, bf16[128,1024]{1,0:T(8,128)(2,1)}, f32[2,128]{1,0:T(2,128)}, bf16[1,64,384]{2,1,0:T(8,128)(2,1)}, bf16[1,64...) custom-call(bf16[128,1024]{1,0:T(8,128)(2,1)} %get-tuple-element.18.refs_0_, ...), custom_call_target="tpu_custom_call" | custom-call | tf_op jit(solution)/shard_map/pallas_call | solution.py:522

commit v5 on v4

--- a/solution.py
+++ b/solution.py
@@ -120,15 +120,12 @@
 
     def ag_copy(q, flow, zz, core):
         at = gathered[q].at[2 * zz + c]
-        return remote(
-            at, at, ag_send.at[flow, zz, q], arrival.at[2 * zz + c, q], along_z(beside[flow], core)
-        )
+        place = jnp.where(core == c, zz, nz)
+        return remote(at, at, ag_send.at[q], arrival.at[place, q], along_z(beside[flow], core))
 
     def pass_copy(q, zz):
         at = gathered[q].at[2 * zz + c]
-        return remote(
-            at, at, pass_send.at[lax.rem(zz, NZL), q], arrival.at[2 * zz + c, q], other
-        )
+        return remote(at, at, pass_send.at[q], arrival.at[nz, q], other)
 
     def onward(q, flow, s, zz):
         if s + 1 < NZL - 1:
@@ -247,22 +244,16 @@
     for s in range(3, NZL + 1):
         forward(s)
 
-    def passed(b, _):
-        for q in range(3):
-            place = first_own + 2 * b + 1 - c
-            at = gathered[q].at[place]
-            pltpu.make_async_copy(at, at, arrival.at[place, q]).wait()
-        return 0
-
-    lax.fori_loop(0, NZL, passed, 0)
+    def all_of(ref, sem, count):
+        part = ref.at[pl.ds(0, count)]
+        pltpu.make_async_copy(part, part, sem).wait()
+
+    for q in range(3):
+        all_of(gathered[q], arrival.at[nz, q], NZL)
 
     shard_rows = down_in.shape[1]
     for i in range(nz):
         down_full[i * shard_rows : (i + 1) * shard_rows] = all_d[first_own + i]
-
-    def all_of(ref, sem, count):
-        part = ref.at[pl.ds(0, count)]
-        pltpu.make_async_copy(part, part, sem).wait()
 
     all_of(recv_rows, a2a_recv, planes - 1)
 
@@ -306,7 +297,7 @@
 
     def push_copy(q, zz):
         at, b = parts[q].at[2 * zz + 1 - c], lax.rem(zz, NZL)
-        return remote(at, at, push_send.at[b, q], push_recv.at[b, q], other)
+        return remote(at, at, push_send.at[q], push_recv.at[b, q], other)
 
     def pushed(q, zz):
         @pl.when(family(zz) != c)
@@ -314,44 +305,41 @@
             at = parts[q].at[2 * zz + c]
             pltpu.make_async_copy(at, at, push_recv.at[lax.rem(zz, NZL), q]).wait()
 
-    def first_copy(q, flow, h, core):
+    def first_copy(q, flow, core):
         zz = target(flow, far(flow, core))
         return family(zz) == c, remote(
-            parts[q].at[2 * zz + core], sums[q].at[flow, zz], rs_first.at[flow, h, q],
+            parts[q].at[2 * zz + core], sums[q].at[flow, zz], rs_first.at[q],
             rs_recv.at[flow, zz, q], along_z(beside[flow], core),
         )
 
     for q in range(3):
         for flow in (0, 1):
-            for h, core in enumerate((c, 1 - c)):
-                ours, copy = first_copy(q, flow, h, core)
+            for core in (c, 1 - c):
+                ours, copy = first_copy(q, flow, core)
                 pl.when(ours)(copy.start)
 
-    def each_push(do):
-        def some(s, _):
-            for q in range(3):
-                for flow in (0, 1):
-                    left = far(flow, 1 - c) - s
-                    zz = target(flow, left)
-
-                    @pl.when((family(zz) == c) & (left > 0))
-                    def _(q=q, zz=zz):
-                        do(push_copy(q, zz))
-
-            return 0
-
-        lax.fori_loop(1, NZL, some, 0)
-
-        @pl.when(zh == c)
-        def _():
-            for q in range(3):
-                do(push_copy(q, z))
-
-    each_push(lambda copy: copy.start())
+    def push(s, _):
+        for q in range(3):
+            for flow in (0, 1):
+                left = far(flow, 1 - c) - s
+                zz = target(flow, left)
+
+                @pl.when((family(zz) == c) & (left > 0))
+                def _(q=q, zz=zz):
+                    push_copy(q, zz).start()
+
+        return 0
+
+    lax.fori_loop(1, NZL, push, 0)
+
+    @pl.when(zh == c)
+    def _():
+        for q in range(3):
+            push_copy(q, z).start()
 
     def rs_copy(q, flow, zz, src):
         return remote(
-            src, sums[q].at[flow, zz], rs_send.at[flow, zz, q], rs_recv.at[flow, zz, q], ring[flow]
+            src, sums[q].at[flow, zz], rs_send.at[q], rs_recv.at[flow, zz, q], ring[flow]
         )
 
     def summing(left):
@@ -399,10 +387,15 @@
         lax.fori_loop(0, per, send, 0)
         return 0
 
-    lax.fori_loop(0, tiles, outer, 0)
+    left = NZL - 1
+    for t in range(tiles):
+        outer(t, 0)
+        if left > 0:
+            summing(left)
+            left -= 1
     recv_back[me] = send_back[me]
-    for left in range(NZL - 1, 0, -1):
-        summing(left)
+    for hops in range(left, 0, -1):
+        summing(hops)
 
     all_of(recv_back, back_recv, planes - 1)
     p0, p1 = (picks(k, 0, slots) for k in range(2))
@@ -424,34 +417,30 @@
             total += sums[q][flow, z].astype(F32)
         outs[q][0] = (total * (1.0 / nz)).astype(BF)
 
-    def sent(s, _):
-        for q in range(3):
-            for flow in (0, 1):
-                zz = source(flow, s)
-
-                @pl.when(s < far(flow, c))
-                def _(q=q, flow=flow, zz=zz):
-                    ag_copy(q, flow, zz, c).wait_send()
-
-                    @pl.when((family(zz) != c) & ((s > 0) | (flow == 0)))
-                    def _():
-                        pass_copy(q, zz).wait_send()
-
-                zz = target(flow, s + 1)
-
-                @pl.when(s + 1 < far(flow, c))
-                def _(q=q, flow=flow, zz=zz):
-                    rs_copy(q, flow, zz, sums[q].at[flow, zz]).wait_send()
-
-        return 0
-
-    lax.fori_loop(0, NZL, sent, 0)
-    each_push(lambda copy: copy.wait_send())
+    def count(flags):
+        return sum(jnp.where(flag, 1, 0) for flag in flags)
+
+    def drain(sem, number, least, most):
+        for n in range(max(least, 1), most + 1):
+
+            @pl.when(number == n)
+            def _(n=n):
+                for q in range(3):
+                    all_of(gathered[q], sem.at[q], n)
+
+    ends = [family(source(flow, far(flow, c))) != c for flow in (0, 1)]
+    firsts = {core: [first_copy(0, flow, core)[0] for flow in (0, 1)] for core in (0, 1)}
+    drain(pass_send, NZL - count(ends), NZL - 2, NZL)
+    drain(
+        push_send,
+        NZL - count(family(target(flow, far(flow, 1 - c))) == c for flow in (0, 1)),
+        NZL - 2,
+        NZL,
+    )
+    drain(rs_first, count(firsts[0] + firsts[1]), 0, 4)
     for q in range(3):
-        for flow in (0, 1):
-            for h, core in enumerate((c, 1 - c)):
-                ours, copy = first_copy(q, flow, h, core)
-                pl.when(ours)(copy.wait_send)
+        all_of(gathered[q], ag_send.at[q], 2 * NZL - 1)
+        all_of(gathered[q], rs_send.at[q], 2 * NZL - 3)
     all_of(send_rows, a2a_send, planes - 1)
     all_of(send_back, back_send, planes - 1)
 
@@ -496,13 +485,13 @@
             *(pltpu.VMEM((2, nz, *s), BF) for s in shapes),
             dma((2,)),
             dma((3,)),
+            dma((3,)),
+            dma((nz + 1, 3)),
+            dma((3,)),
+            dma((3,)),
             dma((2, nz, 3)),
-            dma((2 * nz, 3)),
-            dma((NZL, 3)),
-            dma((2, nz, 3)),
-            dma((2, nz, 3)),
-            dma((2, 2, 3)),
-            dma((NZL, 3)),
+            dma((3,)),
+            dma((3,)),
             dma((NZL, 3)),
             dma,
             dma,

time: 88.4 us -> 85.4 us (0.966)
  the two profiles are of different devices: /device:TPU:2 before, /device:TPU:1 now
where the time goes in v5:
time: 85.4 us; the launch traced here: 84.1 us
  Pallas kernels  82.8 us (97%)
  between operations  1.29 us (2%)
    pallas_call x1, Pallas kernels, shards(): pl.pallas_call(kernel, out_shape=(jax.ShapeDtypeStruct((rows_tok, width),...  80.9 us
    pallas_call x1, Pallas kernels, shards(): pl.pallas_call(hand_over, out_shape=tuple((jax.ShapeDtypeStruct(o.shape,...  1.92 us

profile of v5, /device:TPU:1, one launch (start us, length us, event | category | flops | bytes accessed | tf_op | source)
XLA Modules:
  0.0 84.1 jit_solution(17657041735519711603)
XLA Ops:
  1.3 80.9 %shard_map.127 = (bf16[128,1024]{1,0:T(8,128)(2,1)}, bf16[128,1024]{1,0:T(8,128)(2,1)}, f32[2,128]{1,0:T(2,128)}, bf16[1,64,384]{2,1,0:T(8,128)(2,1)}, bf16[1,64...) custom-call(bf16[128,1024]{1,0:T(8,128)(2,1)} %tok_in.1, bf16[128,1024]{1,0:T(8,128)(2,1)} %cot_in.1, s32[2,128]{1,0:T(2,128)} %bitcast.3, ...), custom_call_target="tpu_custom_call" | custom-call | flops 3623878656 | bytes 2097152 | tf_op jit(solution)/shard_map/pallas_call | solution.py:467
  82.2 1.9 %shard_map.128 = (bf16[128,1024]{1,0:T(8,128)(2,1)}, bf16[128,1024]{1,0:T(8,128)(2,1)}, f32[2,128]{1,0:T(2,128)}, bf16[1,64,384]{2,1,0:T(8,128)(2,1)}, bf16[1,64...) custom-call(bf16[128,1024]{1,0:T(8,128)(2,1)} %get-tuple-element.18.refs_0_, ...), custom_call_target="tpu_custom_call" | custom-call | tf_op jit(solution)/shard_map/pallas_call | solution.py:511
